TPU v7x, 32 devices: a whole 2x2x4 slice. The times are simulated.
32 devices in a mesh: dp: 8 (over z, x), fsdp: 4 (over y, core).
Axes of the slice: x: 2, y: 2, z: 4, core: 2. Of those that a mesh axis runs over, the one named last changes fastest.
Arguments:
- inputs: bfloat16 [64, 529, 768], P(('dp', 'fsdp')), may hold values from -6 to 6
- row_kind: int32 [64], P(('dp', 'fsdp')), may hold values from 0 to 1
- ln1_gain: bfloat16 [768], P(('dp', 'fsdp')), may hold values from 0.25 to 1.75
- ln1_bias: bfloat16 [768], P(('dp', 'fsdp')), may hold values from -1.75 to 1.75
- w_qkv: bfloat16 [768, 2304], P(('dp', 'fsdp')), may hold values from -0.21875 to 0.21875
- b_query: bfloat16 [768], P(('dp', 'fsdp')), may hold values from -3 to 3
- b_value: bfloat16 [768], P(('dp', 'fsdp')), may hold values from -3 to 3
- w_out: bfloat16 [768, 768], P(('dp', 'fsdp')), may hold values from -1.75 to 1.75
- b_out: bfloat16 [768], P(('dp', 'fsdp')), may hold values from -1.75 to 1.75
- ln2_gain: bfloat16 [768], P(('dp', 'fsdp')), may hold values from 0.25 to 1.75
- ln2_bias: bfloat16 [768], P(('dp', 'fsdp')), may hold values from -1.75 to 1.75
- w_up: bfloat16 [768, 3072], P(('dp', 'fsdp')), may hold values from -0.21875 to 0.21875
- b_up: bfloat16 [3072], P(('dp', 'fsdp')), may hold values from -3 to 3
- w_down: bfloat16 [3072, 768], P(('dp', 'fsdp')), may hold values from -0.109375 to 0.109375
- b_down: bfloat16 [768], P(('dp', 'fsdp')), may hold values from -1.75 to 1.75
- out_grad: bfloat16 [64, 529, 768], P(('dp', 'fsdp')), may hold values from -6 to 6
Outputs:
- outputs: bfloat16 [64, 529, 768], P(('dp', 'fsdp'))
- input_grad: bfloat16 [64, 529, 768], P(('dp', 'fsdp'))
- grad_ln1_gain: float32 [768], P(('dp', 'fsdp'))
- grad_ln1_bias: float32 [768], P(('dp', 'fsdp'))
- grad_w_qkv: float32 [768, 2304], P(('dp', 'fsdp'))
- grad_b_query: float32 [768], P(('dp', 'fsdp'))
- grad_b_value: float32 [768], P(('dp', 'fsdp'))
- grad_w_out: float32 [768, 768], P(('dp', 'fsdp'))
- grad_b_out: float32 [768], P(('dp', 'fsdp'))
- grad_ln2_gain: float32 [768], P(('dp', 'fsdp'))
- grad_ln2_bias: float32 [768], P(('dp', 'fsdp'))
- grad_w_up: float32 [768, 3072], P(('dp', 'fsdp'))
- grad_b_up: float32 [3072], P(('dp', 'fsdp'))
- grad_w_down: float32 [3072, 768], P(('dp', 'fsdp'))
- grad_b_down: float32 [768], P(('dp', 'fsdp'))
Inputs may be any that keep to these rules, and one draw needn't show every extreme that they name: `row_kind`: 0 marks a row holding one strip of 529 patches; 1 marks a row holding two half strips of 264 patches followed by one padding slot.
All inputs are finite; a program needn't handle non-finite values.
Results may differ from a plain program's by a relative error of at most 0.012.
Values may be sent and summed in bfloat16 or wider, within the bound.
A program may use at most 256 MiB of HBM per device.

v0:
```python
import math

import jax
import jax.numpy as jnp
from jax import lax
from jax.sharding import PartitionSpec as P

HEAD_DIM = 64
SEQ = 529
HALF = 264


EPSILON = 1e-06


def segments(row_kind, seq_len, half_len):
    position = jnp.arange(seq_len, dtype=jnp.int32)
    packed = jnp.where(position < half_len, 0, jnp.where(position < 2 * half_len, 1, 2)).astype(
        jnp.int32
    )
    return jnp.where(row_kind[:, None] == 1, packed[None, :], 0)


def normalize(values, norm_gain, norm_shift):
    row_mean = jnp.mean(values, -1, keepdims=True)
    centred = values - row_mean
    inverse = lax.rsqrt(jnp.mean(centred * centred, -1, keepdims=True) + EPSILON)
    normed = centred * inverse
    return (normed, inverse, (normed * norm_gain + norm_shift).astype(jnp.bfloat16))


def normalize_back(grad_out, normed, inverse, norm_gain):
    scaled = grad_out * norm_gain
    return inverse * (
        scaled
        - jnp.mean(scaled, -1, keepdims=True)
        - normed * jnp.mean(scaled * normed, -1, keepdims=True)
    )


def exact_gelu(values):
    return jax.nn.gelu(values, approximate=False)


def masked_scores(query_rows, key_rows, same):
    scale = 1.0 / math.sqrt(query_rows.shape[-1])
    scores = (
        jnp.einsum("bqhd,bkhd->bhqk", query_rows, key_rows, preferred_element_type=jnp.float32)
        * scale
    )
    return jnp.where(same, scores, -1e30)


def attention_forward(activations, segment, weights, row_count):
    w_qkv, w_out, b_query, b_value, b_out, norm_gain, norm_shift = weights
    model_width = activations.shape[1]
    normed, inverse, normed_in = normalize(
        activations, norm_gain.astype(jnp.float32), norm_shift.astype(jnp.float32)
    )
    qkv_bias = jnp.concatenate(
        [
            b_query.astype(jnp.float32),
            jnp.zeros(b_query.shape, jnp.float32),
            b_value.astype(jnp.float32),
        ]
    )
    projected = (jnp.dot(normed_in, w_qkv, preferred_element_type=jnp.float32) + qkv_bias).astype(
        jnp.bfloat16
    )
    split = projected.reshape(row_count, -1, 3, model_width // HEAD_DIM, HEAD_DIM)
    query_rows, key_rows, value_rows = (split[:, :, 0], split[:, :, 1], split[:, :, 2])
    same = (segment[:, :, None] == segment[:, None, :])[:, None]
    scores = masked_scores(query_rows, key_rows, same)
    row_max = jnp.max(scores, -1, keepdims=True)
    log_total = row_max + jnp.log(jnp.sum(jnp.exp(scores - row_max), -1, keepdims=True))
    attention_probs = jnp.exp(scores - log_total).astype(jnp.bfloat16)
    mixed = jnp.einsum(
        "bhqk,bkhd->bqhd", attention_probs, value_rows, preferred_element_type=jnp.float32
    )
    mixed = mixed.astype(jnp.bfloat16).reshape(-1, model_width)
    middle = (
        activations
        + jnp.dot(mixed, w_out, preferred_element_type=jnp.float32)
        + b_out.astype(jnp.float32)
    )
    return (
        normed,
        inverse,
        normed_in,
        query_rows,
        key_rows,
        value_rows,
        same,
        log_total,
        mixed,
        middle,
    )


def feedforward_forward(middle, weights):
    w_up, w_down, b_up, b_down, norm_gain, norm_shift = weights
    normed, inverse, normed_mid = normalize(
        middle, norm_gain.astype(jnp.float32), norm_shift.astype(jnp.float32)
    )
    up_proj = jnp.dot(normed_mid, w_up, preferred_element_type=jnp.float32) + b_up.astype(
        jnp.float32
    )
    hidden = exact_gelu(up_proj).astype(jnp.bfloat16)
    result = (
        middle
        + jnp.dot(hidden, w_down, preferred_element_type=jnp.float32)
        + b_down.astype(jnp.float32)
    )
    return (normed, inverse, normed_mid, up_proj, hidden, result)


def attention_back(query_rows, key_rows, value_rows, same, log_total, grad_mixed):
    scale = 1.0 / math.sqrt(query_rows.shape[-1])
    scores = masked_scores(query_rows, key_rows, same)
    attention_probs = jnp.exp(scores - log_total)
    grad_probs = jnp.einsum(
        "bqhd,bkhd->bhqk", grad_mixed, value_rows, preferred_element_type=jnp.float32
    )
    row_dot = jnp.sum(attention_probs * grad_probs, -1, keepdims=True)
    grad_scores = (attention_probs * (grad_probs - row_dot)).astype(jnp.bfloat16)
    grad_query = (
        jnp.einsum("bhqk,bkhd->bqhd", grad_scores, key_rows, preferred_element_type=jnp.float32)
        * scale
    )
    grad_key = (
        jnp.einsum("bhqk,bqhd->bkhd", grad_scores, query_rows, preferred_element_type=jnp.float32)
        * scale
    )
    grad_value = jnp.einsum(
        "bhqk,bqhd->bkhd",
        attention_probs.astype(jnp.bfloat16),
        grad_mixed,
        preferred_element_type=jnp.float32,
    )
    return (grad_query, grad_key, grad_value)


def on_device(
    inputs,
    row_kind,
    ln1_gain,
    ln1_bias,
    w_qkv,
    b_query,
    b_value,
    w_out,
    b_out,
    ln2_gain,
    ln2_bias,
    w_up,
    b_up,
    w_down,
    b_down,
    out_grad,
):
    row_count, seq_len, model_width = inputs.shape
    segment = segments(row_kind, SEQ, HALF)
    activations = inputs.reshape(-1, model_width).astype(jnp.float32)
    attention_set = (
        lax.all_gather(w_qkv, ("dp", "fsdp"), axis=0, tiled=True),
        lax.all_gather(w_out, ("dp", "fsdp"), axis=0, tiled=True),
        lax.all_gather(b_query, ("dp", "fsdp"), axis=0, tiled=True),
        lax.all_gather(b_value, ("dp", "fsdp"), axis=0, tiled=True),
        lax.all_gather(b_out, ("dp", "fsdp"), axis=0, tiled=True),
        lax.all_gather(ln1_gain, ("dp", "fsdp"), axis=0, tiled=True),
        lax.all_gather(ln1_bias, ("dp", "fsdp"), axis=0, tiled=True),
    )
    first = attention_forward(activations, segment, attention_set, row_count)
    feedforward_set = (
        lax.all_gather(w_up, ("dp", "fsdp"), axis=0, tiled=True),
        lax.all_gather(w_down, ("dp", "fsdp"), axis=0, tiled=True),
        lax.all_gather(b_up, ("dp", "fsdp"), axis=0, tiled=True),
        lax.all_gather(b_down, ("dp", "fsdp"), axis=0, tiled=True),
        lax.all_gather(ln2_gain, ("dp", "fsdp"), axis=0, tiled=True),
        lax.all_gather(ln2_bias, ("dp", "fsdp"), axis=0, tiled=True),
    )
    second = feedforward_forward(first[-1], feedforward_set)
    outputs = second[-1].astype(jnp.bfloat16).reshape(row_count, seq_len, model_width)
    attention_set = (
        lax.all_gather(w_qkv, ("dp", "fsdp"), axis=0, tiled=True),
        lax.all_gather(w_out, ("dp", "fsdp"), axis=0, tiled=True),
        lax.all_gather(b_query, ("dp", "fsdp"), axis=0, tiled=True),
        lax.all_gather(b_value, ("dp", "fsdp"), axis=0, tiled=True),
        lax.all_gather(b_out, ("dp", "fsdp"), axis=0, tiled=True),
        lax.all_gather(ln1_gain, ("dp", "fsdp"), axis=0, tiled=True),
        lax.all_gather(ln1_bias, ("dp", "fsdp"), axis=0, tiled=True),
    )
    first = attention_forward(activations, segment, attention_set, row_count)
    feedforward_set = (
        lax.all_gather(w_up, ("dp", "fsdp"), axis=0, tiled=True),
        lax.all_gather(w_down, ("dp", "fsdp"), axis=0, tiled=True),
        lax.all_gather(b_up, ("dp", "fsdp"), axis=0, tiled=True),
        lax.all_gather(b_down, ("dp", "fsdp"), axis=0, tiled=True),
        lax.all_gather(ln2_gain, ("dp", "fsdp"), axis=0, tiled=True),
        lax.all_gather(ln2_bias, ("dp", "fsdp"), axis=0, tiled=True),
    )
    second = feedforward_forward(first[-1], feedforward_set)
    full_qkv, full_out = (attention_set[0], attention_set[1])
    gain_first = attention_set[5].astype(jnp.float32)
    full_up, full_down = (feedforward_set[0], feedforward_set[1])
    gain_second = feedforward_set[4].astype(jnp.float32)
    (
        normed_first,
        inverse_first,
        normed_in,
        query_rows,
        key_rows,
        value_rows,
        same,
        log_total,
        mixed,
        middle,
    ) = first
    normed_second, inverse_second, normed_mid, up_proj, hidden, result = second
    cotangent = out_grad.reshape(-1, model_width)
    grad_w_down = jnp.einsum("nf,nd->fd", hidden, cotangent, preferred_element_type=jnp.float32)
    grad_b_down = jnp.sum(cotangent.astype(jnp.float32), 0)
    grad_hidden = jnp.einsum("nd,fd->nf", cotangent, full_down, preferred_element_type=jnp.float32)
    gelu_pull = jax.vjp(exact_gelu, up_proj)[1]
    grad_up = gelu_pull(grad_hidden)[0].astype(jnp.bfloat16)
    grad_w_up = jnp.einsum("nd,nf->df", normed_mid, grad_up, preferred_element_type=jnp.float32)
    grad_b_up = jnp.sum(grad_up.astype(jnp.float32), 0)
    grad_mid = jnp.einsum("nf,df->nd", grad_up, full_up, preferred_element_type=jnp.float32)
    grad_ln2_gain = jnp.sum(grad_mid * normed_second, 0)
    grad_ln2_bias = jnp.sum(grad_mid, 0)
    grad_middle = cotangent.astype(jnp.float32) + normalize_back(
        grad_mid, normed_second, inverse_second, gain_second
    )
    feedforward_shards = ()
    grad_branch = grad_middle.astype(jnp.bfloat16)
    grad_w_out = jnp.einsum("nd,ne->de", mixed, grad_branch, preferred_element_type=jnp.float32)
    grad_b_out = jnp.sum(grad_branch.astype(jnp.float32), 0)
    grad_mixed = jnp.einsum("ne,de->nd", grad_branch, full_out, preferred_element_type=jnp.float32)
    grad_mixed = grad_mixed.astype(jnp.bfloat16).reshape(query_rows.shape)
    grad_query, grad_key, grad_value = attention_back(
        query_rows, key_rows, value_rows, same, log_total, grad_mixed
    )
    grad_qkv = (
        jnp.stack([grad_query, grad_key, grad_value], 2)
        .reshape(-1, 3 * model_width)
        .astype(jnp.bfloat16)
    )
    grad_w_qkv = jnp.einsum("nd,ne->de", normed_in, grad_qkv, preferred_element_type=jnp.float32)
    grad_b_query = jnp.sum(grad_qkv[:, :model_width].astype(jnp.float32), 0)
    grad_b_value = jnp.sum(grad_qkv[:, 2 * model_width :].astype(jnp.float32), 0)
    grad_normed_in = jnp.einsum("ne,de->nd", grad_qkv, full_qkv, preferred_element_type=jnp.float32)
    grad_ln1_gain = jnp.sum(grad_normed_in * normed_first, 0)
    grad_ln1_bias = jnp.sum(grad_normed_in, 0)
    grad_input = grad_middle + normalize_back(
        grad_normed_in, normed_first, inverse_first, gain_first
    )
    input_grad = grad_input.astype(jnp.bfloat16).reshape(row_count, seq_len, model_width)
    every_shard = (
        lax.psum_scatter(grad_ln1_gain, ("dp", "fsdp"), scatter_dimension=0, tiled=True),
        lax.psum_scatter(grad_ln1_bias, ("dp", "fsdp"), scatter_dimension=0, tiled=True),
        lax.psum_scatter(grad_w_qkv, ("dp", "fsdp"), scatter_dimension=0, tiled=True),
        lax.psum_scatter(grad_b_query, ("dp", "fsdp"), scatter_dimension=0, tiled=True),
        lax.psum_scatter(grad_b_value, ("dp", "fsdp"), scatter_dimension=0, tiled=True),
        lax.psum_scatter(grad_w_out, ("dp", "fsdp"), scatter_dimension=0, tiled=True),
        lax.psum_scatter(grad_b_out, ("dp", "fsdp"), scatter_dimension=0, tiled=True),
        lax.psum_scatter(grad_ln2_gain, ("dp", "fsdp"), scatter_dimension=0, tiled=True),
        lax.psum_scatter(grad_ln2_bias, ("dp", "fsdp"), scatter_dimension=0, tiled=True),
        lax.psum_scatter(grad_w_up, ("dp", "fsdp"), scatter_dimension=0, tiled=True),
        lax.psum_scatter(grad_b_up, ("dp", "fsdp"), scatter_dimension=0, tiled=True),
        lax.psum_scatter(grad_w_down, ("dp", "fsdp"), scatter_dimension=0, tiled=True),
        lax.psum_scatter(grad_b_down, ("dp", "fsdp"), scatter_dimension=0, tiled=True),
    )
    attention_shards = every_shard[:7]
    feedforward_shards = every_shard[7:]
    return (
        outputs,
        input_grad,
        attention_shards[0],
        attention_shards[1],
        attention_shards[2],
        attention_shards[3],
        attention_shards[4],
        attention_shards[5],
        attention_shards[6],
        feedforward_shards[0],
        feedforward_shards[1],
        feedforward_shards[2],
        feedforward_shards[3],
        feedforward_shards[4],
        feedforward_shards[5],
    )


def solution(mesh):
    in_specs = (
        P(("dp", "fsdp"), None, None),
        P(("dp", "fsdp")),
        P(("dp", "fsdp")),
        P(("dp", "fsdp")),
        P(("dp", "fsdp"), None),
        P(("dp", "fsdp")),
        P(("dp", "fsdp")),
        P(("dp", "fsdp"), None),
        P(("dp", "fsdp")),
        P(("dp", "fsdp")),
        P(("dp", "fsdp")),
        P(("dp", "fsdp"), None),
        P(("dp", "fsdp")),
        P(("dp", "fsdp"), None),
        P(("dp", "fsdp")),
        P(("dp", "fsdp"), None, None),
    )
    out_specs = (
        P(("dp", "fsdp"), None, None),
        P(("dp", "fsdp"), None, None),
        P(("dp", "fsdp")),
        P(("dp", "fsdp")),
        P(("dp", "fsdp"), None),
        P(("dp", "fsdp")),
        P(("dp", "fsdp")),
        P(("dp", "fsdp"), None),
        P(("dp", "fsdp")),
        P(("dp", "fsdp")),
        P(("dp", "fsdp")),
        P(("dp", "fsdp"), None),
        P(("dp", "fsdp")),
        P(("dp", "fsdp"), None),
        P(("dp", "fsdp")),
    )
    return jax.shard_map(
        on_device, mesh=mesh, in_specs=in_specs, out_specs=out_specs, check_vma=False
    )
```

profile of v0, /device:TPU:0, one launch (start us, length us, event | category | flops | bytes accessed | tf_op | source)
XLA Modules:
  0.0 851.9 jit_solution(4560029318459708499)
XLA Ops:
  10.0 2.8 convert_reduce_fusion.5
  13.1 8.6 %multiply_reduce_fusion.6 = f32[2,529]{0,1:T(8,128)S(1)} fusion(bf16[2,529,768]{2,0,1:T(2,128)(2,1)} %param.16, f32[2,529]{0,1:T(8,128)S(1)} %broadcast_multiply_fusion), kind=kLoop, calls=%fused_computation.52 | loop fusion | flops 3249118 | bytes 1633552 | tf_op jit(solution)/shard_map/reduce_sum | solution.py:27
  25.7 43.3 %all-reduce.19 = (bf16[768]{0:T(1024)(128)(2,1)S(1)}, bf16[768]{0:T(1024)(128)(2,1)S(1)}, bf16[768]{0:T(1024)(128)(2,1)S(1)}, bf16[768]{0:T(1024)(128)(2,1)S(1)}...) all-reduce(bf16[768]{0:T(1024)(128)(2,1)S(1)} %dynamic-update-slice, ...), channel_id=1, replica_groups=mesh['dp'=8,'fsdp'=4] {'dp','fsdp'}, use_global_device_ids=true, to_apply=%add.3 | all-reduce | flops 9216 | bytes 36864
  70.0 2.9 add_convert_fusion.4
  77.8 3.9 reshape.224
  81.8 9.5 %fusion.8 = bf16[1058,2304]{1,0:T(8,128)(2,1)} fusion(bf16[768,2304]{1,0:T(8,128)(2,1)} %all-gather.5.cloned.1.call-done, f32[2304]{0:T(1024)S(1)} %pad_maximum_fusion, f32[1058,768]{1,0:T(8,128)} %reshape.224, f32[768]{0:T(1024)S(1)} %convert_element_type.135, f32[768]{0:T(1024)S(1)} %convert_element_type.134, f32[1058]{0:T(1024)S(1)} %rsqrt.23, ...), kind=kOutput, calls=%fused_computation.28 | convolution fusion | flops 3753140736 | bytes 11688208 | tf_op jit(solution)/shard_map/dot_general | solution.py:67
  91.2 15.7 %reshape.243 = bf16[2,529,3,12,64]{4,3,2,1,0:T(8,128)(2,1)} reshape(bf16[1058,2304]{1,0:T(8,128)(2,1)} %fusion.8) | data formatting | bytes 9750528 | tf_op jit(solution)/shard_map/reshape | solution.py:70
  106.9 9.3 %fusion.38 = (bf16[2,529,1,12,64]{4,3,2,1,0:T(8,128)(2,1)}, bf16[2,529,1,12,64]{4,3,2,1,0:T(8,128)(2,1)}, bf16[2,529,1,12,64]{4,3,2,1,0:T(8,128)(2,1)}) fusion(bf16[2,529,3,12,64]{4,3,2,1,0:T(8,128)(2,1)} %reshape.243), kind=kLoop, calls=%fused_computation.96 | loop fusion | bytes 9750528 | tf_op jit(solution)/shard_map/slice | solution.py:71
  116.2 5.3 copy.115
  121.6 7.0 copy.114
  128.5 6.3 copy.116
  134.8 15.2 %fusion = (f32[2,12,529]{2,1,0:T(8,128)S(1)}, f32[2,12,529,529]{2,3,1,0:T(8,128)}) fusion(pred[2,529,529]{1,2,0:T(8,128)(4,1)S(1)} %broadcast_compare_fusion, bf16[2,529,1,12,64]{1,4,3,0,2:T(8,128)(2,1)} %copy.116, bf16[2,529,1,12,64]{1,4,3,0,2:T(8,128)(2,1)S(1)} %copy.115), kind=kOutput, calls=%fused_computation.5 | convolution fusion | flops 879807360 | bytes 30725378 | tf_op jit(solution)/shard_map/bqhd,bkhd->bhqk/dot_general | solution.py:48
  150.0 14.5 %exponential_reduce_fusion = f32[2,12,529]{2,1,0:T(8,128)S(1)} fusion(f32[2,12,529,529]{2,3,1,0:T(8,128)} %get-tuple-element.111, f32[2,12,529]{2,1,0:T(8,128)S(1)} %get-tuple-element.110, pred[2,529,529]{1,2,0:T(8,128)(4,1)S(1)} %broadcast_compare_fusion), kind=kLoop, calls=%fused_computation.3 | loop fusion | flops 26852040 | bytes 27525986 | tf_op jit(solution)/shard_map/reduce_sum | solution.py:75
  164.6 15.7 %convert_bitcast_fusion = bf16[2,529,12,64]{1,3,2,0:T(8,128)(2,1)} fusion(bf16[2,529,1,12,64]{1,4,3,0,2:T(8,128)(2,1)S(1)} %copy-done.6, f32[2,12,529,529]{2,3,1,0:T(8,128)} %get-tuple-element.111, f32[2,12,529]{2,1,0:T(8,128)S(1)} %log_add_fusion, pred[2,529,529]{1,2,0:T(8,128)(4,1)S(1)} %broadcast_compare_fusion), kind=kOutput, calls=%fused_computation.67 | convolution fusion | flops 887348864 | bytes 30725378 | tf_op jit(solution)/shard_map/bhqk,bkhd->bqhd/dot_general | solution.py:77
  180.3 3.6 copy.93
  183.9 2.7 reshape.219
  186.6 4.6 fusion.39
  191.7 3.7 all-gather.9.cloned.1.call-done
  195.5 38.0 %multiply_convert_fusion.1 = (bf16[1058,3072]{1,0:T(8,128)(2,1)}, f32[1058,3072]{1,0:T(8,128)}, f32[1058,3072]{1,0:T(8,128)}) fusion(f32[3072]{0:T(1024)S(1)} %convert_element_type.147, bf16[768,3072]{1,0:T(8,128)(2,1)} %all-gather.9.cloned.1.call-done, f32[1058,768]{1,0:T(8,128)S(1)} %get-tuple-element.113, f32[768]{0:T(1024)S(1)} %convert_element_type.145, ...), kind=kOutput, calls=%fused_computation.13 | convolution fusion | flops 5210844672 | bytes 40497424 | tf_op jit(solution)/shard_map/dot_general | solution.py:105
  233.5 27.2 %all-gather.11.cloned.1.call-done = bf16[3072,768]{1,0:T(8,128)(2,1)} async-done(((bf16[96,768]{1,0:T(8,128)(2,1)}), bf16[3072,768]{1,0:T(8,128)(2,1)}) %all-gather.11.cloned.1.call-update) | async-done | bytes 4718608 | tf_op jit(solution)/shard_map/all_gather | solution.py:176
  260.7 19.3 %convert_reduce_fusion = (f32[3072]{0:T(1024)}, bf16[1058,3072]{1,0:T(8,128)(2,1)}) fusion(f32[1058,3072]{1,0:T(8,128)} %get-tuple-element.106, f32[1058,3072]{1,0:T(8,128)} %get-tuple-element.114, bf16[1058,768]{1,0:T(8,128)(2,1)} %reshape.221, bf16[3072,768]{1,0:T(8,128)(2,1)} %all-gather.11.cloned.1.call-done), kind=kOutput, calls=%fused_computation.11 | convolution fusion | flops 5044270080 | bytes 38857728 | tf_op jit(solution)/shard_map/nd,fd->nf/dot_general | solution.py:223
  280.0 11.0 %multiply_reduce_fusion.1 = (f32[768]{0:T(1024)}, f32[1058]{0:T(1024)S(1)}, f32[1058]{0:T(1024)S(1)}, f32[768]{0:T(1024)}, f32[1058,768]{1,0:T(8,128)S(1)}) fusion(f32[1058,768]{1,0:T(8,128)S(1)} %get-tuple-element.113, f32[1058]{0:T(1024)S(1)} %add_rsqrt_fusion.1, f32[1058]{0:T(1024)S(1)} %broadcast_multiply_fusion.5, f32[768]{0:T(1024)S(1)} %convert_element_type.144, ...), kind=kOutput, calls=%fused_computation.39 | convolution fusion | flops 4999579648 | bytes 17745440 | tf_op jit(solution)/shard_map/nf,df->nd/dot_general | solution.py:228
  294.2 3.1 fusion.29
  297.4 4.9 convolution_convert_fusion
  302.4 6.5 reshape.244
  308.8 6.3 copy.96
  315.1 28.8 %multiply_reduce_fusion = (f32[2,12,529]{2,1,0:T(8,128)S(1)}, f32[2,12,529,529]{2,3,1,0:T(8,128)}) fusion(f32[2,12,529,529]{2,3,1,0:T(8,128)} %get-tuple-element.111, f32[2,12,529]{2,1,0:T(8,128)S(1)} %copy-done.10, pred[2,529,529]{1,2,0:T(8,128)(4,1)} %copy-done.3, bf16[2,529,12,64]{1,3,2,0:T(8,128)(2,1)} %copy.96, bf16[2,529,1,12,64]{1,4,3,0,2:T(8,128)(2,1)} %copy.114), kind=kOutput, calls=%fused_computation.1 | convolution fusion | flops 893239744 | bytes 57640896 | tf_op jit(solution)/shard_map/bqhd,bkhd->bhqk/dot_general | solution.py:121
  343.9 27.8 %multiply_convert_fusion = bf16[2,12,529,529]{2,3,1,0:T(8,128)(2,1)} fusion(f32[2,12,529,529]{2,3,1,0:T(8,128)} %get-tuple-element.117, f32[2,12,529,529]{2,3,1,0:T(8,128)} %get-tuple-element.111, f32[2,12,529]{2,1,0:T(8,128)S(1)} %get-tuple-element.116, f32[2,12,529]{2,1,0:T(8,128)S(1)} %copy-done.10, pred[2,529,529]{1,2,0:T(8,128)(4,1)} %copy-done.3), kind=kLoop, calls=%fused_computation | loop fusion | flops 40297104 | bytes 67823088 | tf_op jit(solution)/shard_map/convert_element_type | solution.py:125
  371.7 10.2 %multiply_bitcast_fusion = bf16[2,529,1,12,64]{1,4,3,0,2:T(8,128)(2,1)} fusion(bf16[2,12,529,529]{2,3,1,0:T(8,128)(2,1)} %multiply_convert_fusion, bf16[2,529,1,12,64]{1,4,3,0,2:T(8,128)(2,1)} %copy-done), kind=kOutput, calls=%fused_computation.33 | convolution fusion | flops 861296640 | bytes 16682544 | tf_op jit(solution)/shard_map/bhqk,bqhd->bkhd/dot_general | solution.py:131
  381.9 10.4 %multiply_bitcast_fusion.1 = bf16[2,529,1,12,64]{1,4,3,0,2:T(8,128)(2,1)} fusion(bf16[2,12,529,529]{2,3,1,0:T(8,128)(2,1)} %multiply_convert_fusion, bf16[2,529,1,12,64]{1,4,3,0,2:T(8,128)(2,1)S(1)} %copy-done.2), kind=kOutput, calls=%fused_computation.34 | convolution fusion | flops 861296640 | bytes 16682544 | tf_op jit(solution)/shard_map/bhqk,bkhd->bqhd/dot_general | solution.py:127
  392.3 16.5 %convolution_bitcast_fusion = bf16[2,529,1,12,64]{1,4,3,0,2:T(8,128)(2,1)} fusion(bf16[2,529,12,64]{1,3,2,0:T(8,128)(2,1)} %copy.96, f32[2,12,529,529]{2,3,1,0:T(8,128)} %get-tuple-element.111, f32[2,12,529]{2,1,0:T(8,128)S(1)} %copy-done.10, pred[2,529,529]{1,2,0:T(8,128)(4,1)} %copy-done.3), kind=kOutput, calls=%fused_computation.57 | convolution fusion | flops 886536320 | bytes 30725378 | tf_op jit(solution)/shard_map/bhqk,bqhd->bkhd/dot_general | solution.py:134
  408.8 3.7 maximum_convert_fusion
  412.5 5.8 copy.101
  418.3 12.3 %convert_element_type.157 = bf16[1058,2304]{0,1:T(8,128)(2,1)} reshape(bf16[2,529,3,12,64]{1,0,4,3,2:T(2,128)(2,1)} %copy.101) | data formatting | bytes 9750528 | tf_op jit(solution)/shard_map/convert_element_type | solution.py:246
  430.5 10.7 %fusion.40 = f32[768,2304]{1,0:T(8,128)} fusion(bf16[1058,768]{1,0:T(8,128)(2,1)} %convert_element_type.160, bf16[1058,2304]{0,1:T(8,128)(2,1)} %convert_element_type.157), kind=kOutput, calls=%fused_computation.98 | convolution fusion | flops 3744202752 | bytes 13578240 | tf_op jit(solution)/shard_map/nd,ne->de/dot_general | solution.py:248
  441.3 12.2 %fusion.36 = f32[768,3072]{1,0:T(8,128)} fusion(bf16[1058,3072]{1,0:T(8,128)(2,1)} %get-tuple-element.120, f32[1058,768]{1,0:T(8,128)S(1)} %get-tuple-element.113, f32[768]{0:T(1024)S(1)} %convert_element_type.145, f32[768]{0:T(1024)S(1)} %convert_element_type.144, f32[1058]{0:T(1024)S(1)} %add_rsqrt_fusion.1, f32[1058]{0:T(1024)S(1)} %broadcast_multiply_fusion.5), kind=kOutput, calls=%fused_computation.95 | convolution fusion | flops 4996333056 | bytes 19202320 | tf_op jit(solution)/shard_map/nd,nf->df/dot_general | solution.py:226
  453.6 11.3 %fusion.41 = f32[3072,768]{1,0:T(8,128)} fusion(bf16[1058,3072]{1,0:T(8,128)(2,1)} %get-tuple-element.105, bf16[1058,768]{1,0:T(8,128)(2,1)} %reshape.221), kind=kOutput, calls=%fused_computation.99 | convolution fusion | flops 4992270336 | bytes 17562624 | tf_op jit(solution)/shard_map/nf,nd->fd/dot_general | solution.py:221
  465.6 2.8 convert_reduce_fusion.4
  468.4 10.2 %fusion.11 = bf16[1058,768]{1,0:T(8,128)(2,1)} fusion(f32[1058,768]{1,0:T(8,128)S(1)} %get-tuple-element.113, bf16[1058,3072]{1,0:T(8,128)(2,1)} %get-tuple-element.105, bf16[3072,768]{1,0:T(8,128)(2,1)} %all-gather.11.cloned.1.call-done, f32[768]{0:T(1024)S(1)} %convert_element_type.149), kind=kOutput, calls=%fused_computation.38 | convolution fusion | flops 4994707968 | bytes 16097280 | tf_op jit(solution)/shard_map/dot_general | solution.py:111
  478.7 3.1 reshape.220
  481.8 4.0 copy.104
  485.9 2.6 convert_reduce_fusion.1
  488.5 9.5 %multiply_reduce_fusion.2 = (f32[768]{0:T(1024)S(1)}, f32[1058]{0:T(1024)S(1)}, f32[1058]{0:T(1024)S(1)}, f32[768]{0:T(1024)S(1)}, f32[1058,768]{1,0:T(8,128)}) fusion(f32[1058,768]{1,0:T(8,128)S(1)} %copy-done.4, f32[1058]{0:T(1024)S(1)} %copy-done.16, f32[1058]{0:T(1024)S(1)} %copy-done.14, f32[768]{0:T(1024)S(1)} %copy-done.12, ...), kind=kOutput, calls=%fused_computation.41 | convolution fusion | flops 3751512064 | bytes 14940704 | tf_op jit(solution)/shard_map/ne,de->nd/dot_general | solution.py:251
  498.0 41.2 %all-reduce.18 = (f32[768]{0:T(1024)S(1)}, f32[768]{0:T(1024)S(1)}, f32[768]{0:T(1024)S(1)}, f32[768]{0:T(1024)S(1)}, f32[768]{0:T(1024)S(1)}, /*index=5*/f32[76...) all-reduce(f32[768]{0:T(1024)S(1)} %get-tuple-element.77, ...), channel_id=2, replica_groups=mesh['dp'=8,'fsdp'=4] {'dp','fsdp'}, use_global_device_ids=true, to_apply=%region_12.13.clone | all-reduce | flops 9216 | bytes 73728
  543.9 4.4 add_convert_fusion.1
  553.0 8.0 reduce-scatter.5.cloned.1.call-done
  561.1 141.5 %reduce-scatter.9.cloned.1.call-done = f32[24,3072]{1,0:T(8,128)} async-done(((f32[768,3072]{1,0:T(8,128)}), f32[24,3072]{1,0:T(8,128)}) %reduce-scatter.9.cloned.1.call-update) | async-done | bytes 294928 | tf_op jit(solution)/shard_map/reduce_scatter | solution.py:268
  702.5 142.1 %reduce-scatter.11.cloned.1.call-done = f32[96,768]{1,0:T(8,128)} async-done(((f32[3072,768]{1,0:T(8,128)}), f32[96,768]{1,0:T(8,128)}) %reduce-scatter.11.cloned.1.call-update) | async-done | bytes 294928 | tf_op jit(solution)/shard_map/reduce_scatter | solution.py:270
  (146 shorter events, 26.8 us)
Async XLA Ops:
  7.2 14.5 %copy-start.1 = (bf16[2,529,768]{2,0,1:T(2,128)(2,1)S(1)}, bf16[2,529,768]{2,0,1:T(2,128)(2,1)}, u32[]{:S(2)}) copy-start(bf16[2,529,768]{2,0,1:T(2,128)(2,1)} %param.16) | copy-start | bytes 4875268
  7.2 74.5 %all-gather.5.cloned.1.call-start = ((), (), s32[]{:S(2)}) async-start(), calls=%async_computation.4 | async-start | bytes 3649536 | tf_op jit(solution)/shard_map/all_gather | solution.py:165
  7.9 178.7 %all-gather.7.cloned.1.call-start = ((), (), s32[]{:S(2)}) async-start(), calls=%async_computation.5 | async-start | bytes 1216512 | tf_op jit(solution)/shard_map/all_gather | solution.py:166
  8.7 186.8 %all-gather.9.cloned.1.call-start = ((), (), s32[]{:S(2)}) async-start(), calls=%async_computation.6 | async-start | bytes 4866048 | tf_op jit(solution)/shard_map/all_gather | solution.py:175
  9.4 251.3 %all-gather.11.cloned.1.call-start = ((), (), s32[]{:S(2)}) async-start(), calls=%async_computation.7 | async-start | bytes 4866048 | tf_op jit(solution)/shard_map/all_gather | solution.py:176
  10.0 543.1 %reduce-scatter.7.cloned.1.call-start = ((), (), s32[]{:S(2)}) async-start(), calls=%async_computation.9 | async-start | bytes 2433024 | tf_op jit(solution)/shard_map/reduce_scatter | solution.py:264
  12.8 10.7 %copy-start.22 = (s32[2]{0:T(128)S(1)}, s32[2]{0:T(128)}, u32[]{:S(2)}) copy-start(s32[2]{0:T(128)} %param.17) | copy-start | bytes 28
  12.8 10.7 %copy-start.23 = (bf16[24]{0:T(256)(128)(2,1)S(1)}, bf16[24]{0:T(256)(128)(2,1)}, u32[]{:S(2)}) copy-start(bf16[24]{0:T(256)(128)(2,1)} %param.25) | copy-start | bytes 148
  12.8 11.0 %copy-start.24 = (bf16[24]{0:T(256)(128)(2,1)S(1)}, bf16[24]{0:T(256)(128)(2,1)}, u32[]{:S(2)}) copy-start(bf16[24]{0:T(256)(128)(2,1)} %param.26) | copy-start | bytes 148
  12.9 11.2 %copy-start.25 = (bf16[24]{0:T(256)(128)(2,1)S(1)}, bf16[24]{0:T(256)(128)(2,1)}, u32[]{:S(2)}) copy-start(bf16[24]{0:T(256)(128)(2,1)} %param.24) | copy-start | bytes 148
  12.9 11.4 %copy-start.26 = (bf16[24]{0:T(256)(128)(2,1)S(1)}, bf16[24]{0:T(256)(128)(2,1)}, u32[]{:S(2)}) copy-start(bf16[24]{0:T(256)(128)(2,1)} %param.18) | copy-start | bytes 148
  12.9 11.7 %copy-start.27 = (bf16[24]{0:T(256)(128)(2,1)S(1)}, bf16[24]{0:T(256)(128)(2,1)}, u32[]{:S(2)}) copy-start(bf16[24]{0:T(256)(128)(2,1)} %param.19) | copy-start | bytes 148
  12.9 11.9 %copy-start.28 = (bf16[24]{0:T(256)(128)(2,1)S(1)}, bf16[24]{0:T(256)(128)(2,1)}, u32[]{:S(2)}) copy-start(bf16[24]{0:T(256)(128)(2,1)} %param.21) | copy-start | bytes 148
  12.9 12.1 %copy-start.29 = (bf16[24]{0:T(256)(128)(2,1)S(1)}, bf16[24]{0:T(256)(128)(2,1)}, u32[]{:S(2)}) copy-start(bf16[24]{0:T(256)(128)(2,1)} %param.22) | copy-start | bytes 148
  12.9 12.3 %copy-start.30 = (bf16[24]{0:T(256)(128)(2,1)S(1)}, bf16[24]{0:T(256)(128)(2,1)}, u32[]{:S(2)}) copy-start(bf16[24]{0:T(256)(128)(2,1)} %param.30) | copy-start | bytes 148
  12.9 12.5 %copy-start.31 = (bf16[96]{0:T(256)(128)(2,1)S(1)}, bf16[96]{0:T(256)(128)(2,1)}, u32[]{:S(2)}) copy-start(bf16[96]{0:T(256)(128)(2,1)} %param.28) | copy-start | bytes 580
  69.1 12.7 %copy-start.11 = (f32[768]{0:T(1024)}, f32[768]{0:T(1024)S(1)}, u32[]{:S(2)}) copy-start(f32[768]{0:T(1024)S(1)} %convert_element_type.134) | copy-start | bytes 9220
  69.2 12.5 %copy-start.13 = (f32[1058]{0:T(1024)}, f32[1058]{0:T(1024)S(1)}, u32[]{:S(2)}) copy-start(f32[1058]{0:T(1024)S(1)} %div.31) | copy-start | bytes 12700
  69.5 12.3 %copy-start.15 = (f32[1058]{0:T(1024)}, f32[1058]{0:T(1024)S(1)}, u32[]{:S(2)}) copy-start(f32[1058]{0:T(1024)S(1)} %rsqrt.23) | copy-start | bytes 12700
  70.0 94.6 %copy-start.3 = (pred[2,529,529]{1,2,0:T(8,128)(4,1)}, pred[2,529,529]{1,2,0:T(8,128)(4,1)S(1)}, u32[]{:S(2)}) copy-start(pred[2,529,529]{1,2,0:T(8,128)(4,1)S(1)} %broadcast_compare_fusion) | copy-start | bytes 1679050
  121.6 13.2 %copy-start = (bf16[2,529,1,12,64]{1,4,3,0,2:T(8,128)(2,1)}, bf16[2,529,1,12,64]{1,4,3,0,2:T(8,128)(2,1)S(1)}, u32[]{:S(2)}) copy-start(bf16[2,529,1,12,64]{1,4,3,0,2:T(8,128)(2,1)S(1)} %copy.115) | copy-start | bytes 4875268
  150.0 14.6 %copy-start.6 = (bf16[2,529,1,12,64]{1,4,3,0,2:T(8,128)(2,1)S(1)}, bf16[2,529,1,12,64]{1,4,3,0,2:T(8,128)(2,1)}, u32[]{:S(2)}) copy-start(bf16[2,529,1,12,64]{1,4,3,0,2:T(8,128)(2,1)} %copy.114) | copy-start | bytes 4875268
  164.6 15.7 %copy-start.9 = (f32[2,12,529]{2,1,0:T(8,128)}, f32[2,12,529]{2,1,0:T(8,128)S(1)}, u32[]{:S(2)}) copy-start(f32[2,12,529]{2,1,0:T(8,128)S(1)} %log_add_fusion) | copy-start | bytes 152356
  280.0 11.0 %copy-start.7 = (bf16[1058,768]{1,0:T(8,128)(2,1)S(1)}, bf16[1058,768]{1,0:T(8,128)(2,1)}, u32[]{:S(2)}) copy-start(bf16[1058,768]{1,0:T(8,128)(2,1)} %reshape.221) | copy-start | bytes 4875268
  291.1 3.2 copy-start.8
  292.5 1.7 copy-start.5
  297.4 263.7 %reduce-scatter.5.cloned.1.call-start = ((), (), s32[]{:S(2)}) async-start(), calls=%async_computation.8 | async-start | bytes 7299072 | tf_op jit(solution)/shard_map/reduce_scatter | solution.py:261
  308.8 6.3 copy-start.10
  371.7 10.2 %copy-start.2 = (bf16[2,529,1,12,64]{1,4,3,0,2:T(8,128)(2,1)S(1)}, bf16[2,529,1,12,64]{1,4,3,0,2:T(8,128)(2,1)}, u32[]{:S(2)}) copy-start(bf16[2,529,1,12,64]{1,4,3,0,2:T(8,128)(2,1)} %copy.116) | copy-start | bytes 4875268
  441.3 261.3 %reduce-scatter.9.cloned.1.call-start = ((), (), s32[]{:S(2)}) async-start(), calls=%async_computation.10 | async-start | bytes 9732096 | tf_op jit(solution)/shard_map/reduce_scatter | solution.py:268
  453.5 391.1 %reduce-scatter.11.cloned.1.call-start = ((), (), s32[]{:S(2)}) async-start(), calls=%async_computation.11 | async-start | bytes 9732096 | tf_op jit(solution)/shard_map/reduce_scatter | solution.py:270
  464.9 0.7 copy-start.20
  478.7 9.8 %copy-start.4 = (f32[1058,768]{1,0:T(8,128)S(1)}, f32[1058,768]{1,0:T(8,128)}, u32[]{:S(2)}) copy-start(f32[1058,768]{1,0:T(8,128)} %reshape.224) | copy-start | bytes 9750532
  478.7 9.8 %copy-start.12 = (f32[768]{0:T(1024)S(1)}, f32[768]{0:T(1024)}, u32[]{:S(2)}) copy-start(f32[768]{0:T(1024)} %copy-done.11) | copy-start | bytes 9220
  478.7 9.8 %copy-start.14 = (f32[1058]{0:T(1024)S(1)}, f32[1058]{0:T(1024)}, u32[]{:S(2)}) copy-start(f32[1058]{0:T(1024)} %copy-done.13) | copy-start | bytes 12700
  478.7 9.8 %copy-start.16 = (f32[1058]{0:T(1024)S(1)}, f32[1058]{0:T(1024)}, u32[]{:S(2)}) copy-start(f32[1058]{0:T(1024)} %copy-done.15) | copy-start | bytes 12700
  481.8 6.6 copy-start.21
  488.5 9.5 %copy-start.17 = (f32[3072]{0:T(1024)S(1)}, f32[3072]{0:T(1024)}, u32[]{:S(2)}) copy-start(f32[3072]{0:T(1024)} %get-tuple-element.119) | copy-start | bytes 36868
  488.5 9.5 %copy-start.18 = (f32[768]{0:T(1024)S(1)}, f32[768]{0:T(1024)}, u32[]{:S(2)}) copy-start(f32[768]{0:T(1024)} %get-tuple-element.75) | copy-start | bytes 9220
  488.5 9.5 %copy-start.19 = (f32[768]{0:T(1024)S(1)}, f32[768]{0:T(1024)}, u32[]{:S(2)}) copy-start(f32[768]{0:T(1024)} %get-tuple-element.83) | copy-start | bytes 9220
Sparse Core Ops, SparseCore 0:
  10.9 63.1 all-gather.4
  77.0 52.9 all-gather.6
  132.9 62.5 all-gather.8
  198.2 62.4 all-gather.10
  297.5 97.8 reduce-scatter.6
  441.4 119.6 reduce-scatter.4
  567.5 134.9 reduce-scatter.8
  710.0 134.6 reduce-scatter.10
where the time goes:
time: 859 us; the launch traced here: 852 us
  waiting for transfers between devices  325 us (38%)
  matrix products  241 us (28%)
  local copies, waits for them, and re-layouts  113 us (13%)
  blocking collectives  84.5 us (10%)
  other arithmetic  72.8 us (8%)
  between operations  15.1 us (2%)
    reduce_scatter x1, waiting for transfers between devices, on_device(): lax.psum_scatter(grad_w_down, ('dp', 'fsdp'), scatter_dimension=0, tiled=...  142 us
    reduce_scatter x1, waiting for transfers between devices, on_device(): lax.psum_scatter(grad_w_up, ('dp', 'fsdp'), scatter_dimension=0, tiled=True)  141 us
    unnamed x2, blocking collectives  84.5 us
    dot_general x1, matrix products, feedforward_forward(): jnp.dot(normed_mid, w_up, preferred_element_type=jnp.float32)  38 us
    unnamed x99, local copies, waits for them, and re-layouts  36.7 us
    dot_general x1, matrix products, attention_back(): jnp.einsum('bqhd,bkhd->bhqk', grad_mixed, value_rows, preferred_element_t...  28.8 us
    convert_element_type x1, other arithmetic, attention_back(): (attention_probs * (grad_probs - row_dot)).astype(jnp.bfloat16)  27.8 us
    all_gather x1, waiting for transfers between devices, on_device(): lax.all_gather(w_down, ('dp', 'fsdp'), axis=0, tiled=True)  27.2 us
  transfers between devices with their start and end apart: 8, of which 5 were waited for; matrix products, arithmetic and copies ran while one was open for 46% of the time, Pallas kernels for 0%

commit v1 on v0

v1 whole, which is shorter than its diff:
```python
import functools
import math

import jax
import jax.numpy as jnp
from jax import lax
from jax.experimental import pallas as pl
from jax.experimental.pallas import tpu as pltpu
from jax.sharding import PartitionSpec as P

D = 768
HD = 64
FF = 3072
SEQ = 529
HALF = 264
EPS = 1e-06
S = 544
T = 2 * S
MB = 272
HG = 4
QW = HG * HD
GW = 3 * QW
FC = 512
OUT_AT = 3 * D
UP_AT = 4 * D
AW = 4 * D + FF
F32 = jnp.float32
BF = jnp.bfloat16
LIMIT = 60 * 2**20
MESH = pl.DeviceIdType.MESH
NN = (((1,), (0,)), ((), ()))
NT = (((1,), (1,)), ((), ()))
TN = (((0,), (0,)), ((), ()))


def mm(a, b, dims=NN):
    return lax.dot_general(a, b, dims, preferred_element_type=F32)


def norm_parts(values):
    mean = jnp.mean(values, -1, keepdims=True)
    centred = values - mean
    inverse = lax.rsqrt(jnp.mean(centred * centred, -1, keepdims=True) + EPS)
    return centred * inverse, inverse


def norm_pull(grad, normed, inverse, gain):
    scaled = grad * gain
    return inverse * (
        scaled
        - jnp.mean(scaled, -1, keepdims=True)
        - normed * jnp.mean(scaled * normed, -1, keepdims=True)
    )


def gelu_both(u):
    a = jnp.abs(u)
    t = 1.0 / (1.0 + (0.3275911 / math.sqrt(2.0)) * a)
    e = jnp.exp(-0.5 * u * u)
    poly = t * (
        0.254829592
        + t * (-0.284496736 + t * (1.421413741 + t * (-1.453152027 + t * 1.061405429)))
    )
    tail = 0.5 * poly * e
    phi = jnp.where(u < 0, tail, 1.0 - tail)
    return u * phi, phi + u * e * (1.0 / math.sqrt(2.0 * math.pi))


def head_lanes(shape, e):
    lane = lax.broadcasted_iota(jnp.int32, shape, 1)
    return (lane // HD) == e


def whole(shape):
    return pl.BlockSpec(shape, lambda *_: (0,) * len(shape))


def rows_of(i):
    return pl.ds(pl.multiple_of(i * MB, 16), MB)


G1, B1, BQ, BV, BO, G2, B2, BD = range(8)


def attn_fwd_kernel(
    kind_ref, x_ref, wg_ref, bqkv_ref, wo_ref, vec_ref,
    h1_ref, qkv_ref, p_ref, attn_ref, rl_ref, x1_ref, fa, fb,
):
    hq, r = pl.program_id(0), pl.program_id(1)

    @pl.when((hq == 0) & (r == 0))
    def _():
        for row in range(2):
            h1_ref[pl.ds(row * S + S - 16, 16), :] = jnp.zeros((16, D), BF)
            n1, _s = norm_parts(x_ref[row].astype(F32))
            h1_ref[pl.ds(row * S, SEQ), :] = (n1 * vec_ref[G1:G1 + 1, :] + vec_ref[B1:B1 + 1, :]).astype(BF)
            slot = lax.broadcasted_iota(jnp.int32, (S, 128), 0)
            lane = lax.broadcasted_iota(jnp.int32, (S, 128), 1)
            packed = jnp.where(slot < HALF, 0, jnp.where(slot < 2 * HALF, 1, 2))
            seg = jnp.where(kind_ref[row] == 1, packed, 0)
            fa[row] = jnp.where((lane < 3) & (seg == lane), -1e30, 0.0).astype(BF)
            fb[row] = jnp.where((lane < 3) & ((seg != lane) | (slot >= SEQ)), 1.0, 0.0).astype(BF)

    @pl.when(r == 0)
    def _():
        @pl.loop(0, T // MB)
        def _(i):
            rows = rows_of(i)
            qkv_ref[rows, :] = (mm(h1_ref[rows, :], wg_ref[...]) + bqkv_ref[...]).astype(BF)

    rows = pl.ds(pl.multiple_of(r * S, 16), S)
    feat_q, feat_k = fa[r], fb[r]
    ones = jnp.ones((S, 128), BF)
    scale = math.log2(math.e) / math.sqrt(HD)
    for j in range(HG // 2):
        at = j * 384
        qp, kp, vp = (qkv_ref[rows, at + 128 * n: at + 128 * (n + 1)] for n in range(3))
        kcat = jnp.concatenate([kp, feat_k], 1)
        total = None
        inv = None
        for e in range(2):
            keep = head_lanes((S, 128), e)
            qcat = jnp.concatenate([jnp.where(keep, qp, jnp.zeros_like(qp)), feat_q], 1)
            s = mm(qcat, kcat, NT)
            m = jnp.max(s, -1, keepdims=True)
            pb = jnp.exp2((s - m) * scale).astype(BF)
            p_ref[0, 2 * j + e] = pb
            vcat = jnp.concatenate([jnp.where(keep, vp, jnp.zeros_like(vp)), ones], 1)
            o = mm(pb, vcat)
            rl = 1.0 / o[:, 128:]
            part = o[:, :128] * rl
            total = part if total is None else total + part
            inv = rl if inv is None else jnp.where(keep, rl, inv)
        out = pl.ds(pl.multiple_of(hq * QW + j * 128, 128), 128)
        attn_ref[rows, out] = total.astype(BF)
        rl_ref[rows, out] = inv

    @pl.when((hq == D // QW - 1) & (r == 1))
    def _():
        for row in range(2):
            x1_ref[pl.ds(row * S + S - 16, 16), :] = jnp.zeros((16, D), F32)
            x1_ref[pl.ds(row * S, SEQ), :] = x_ref[row].astype(F32)

        @pl.loop(0, T // MB)
        def _(i):
            rr = rows_of(i)
            x1_ref[rr, :] = x1_ref[rr, :] + mm(attn_ref[rr, :], wo_ref[...]) + vec_ref[BO:BO + 1, :]


def attn_fwd(kind, x, wide, bqkv, vec):
    return pl.pallas_call(
        attn_fwd_kernel,
        grid=(D // QW, 2),
        in_specs=[
            pl.BlockSpec(memory_space=pltpu.SMEM), whole((2, SEQ, D)),
            pl.BlockSpec((D, GW), lambda h, r: (0, h)), pl.BlockSpec((1, GW), lambda h, r: (0, h)),
            pl.BlockSpec((D, D), lambda h, r: (0, 3)), whole((8, D)),
        ],
        out_specs=[
            whole((T, D)), pl.BlockSpec((T, GW), lambda h, r: (0, h)),
            pl.BlockSpec((1, HG, S, S), lambda h, r: (r, h, 0, 0)),
            whole((T, D)), whole((T, D)), whole((T, D)),
        ],
        out_shape=[
            jax.ShapeDtypeStruct((T, D), BF), jax.ShapeDtypeStruct((T, 3 * D), BF),
            jax.ShapeDtypeStruct((2, D // HD, S, S), BF),
            jax.ShapeDtypeStruct((T, D), BF), jax.ShapeDtypeStruct((T, D), F32), jax.ShapeDtypeStruct((T, D), F32),
        ],
        scratch_shapes=[pltpu.VMEM((2, S, 128), BF), pltpu.VMEM((2, S, 128), BF)],
        compiler_params=pltpu.CompilerParams(vmem_limit_bytes=LIMIT),
        name="attention_forward",
    )(kind, x, wide, bqkv, wide, vec)


def ffn_kernel(
    x1_ref, dm_ref, wu_ref, wd_ref, bu_ref, vec_ref,
    out_ref, dx1_ref, gwu_ref, gwd_ref, gbu_ref, gg2_ref, gb2_ref, gbd_ref,
    h2, h2t, dm, yacc, dacc, gs, dus,
):
    c = pl.program_id(0)

    @pl.when(c == 0)
    def _():
        for row in range(2):
            dm[pl.ds(row * S + S - 16, 16), :] = jnp.zeros((16, D), BF)
            dm[pl.ds(row * S, SEQ), :] = dm_ref[row]

        @pl.loop(0, T // MB)
        def _(i):
            rows = rows_of(i)
            x1 = x1_ref[rows, :]
            n2, _s = norm_parts(x1)
            h2[rows, :] = (n2 * vec_ref[G2:G2 + 1, :] + vec_ref[B2:B2 + 1, :]).astype(BF)
            yacc[rows, :] = x1 + vec_ref[BD:BD + 1, :]
            dacc[rows, :] = jnp.zeros((MB, D), F32)
        h2t[...] = h2[...].T
        gbd_ref[...] = jnp.sum(dm[...].astype(F32), 0, keepdims=True)

    gbu_ref[...] = jnp.zeros_like(gbu_ref)

    @pl.loop(0, T // MB)
    def _(i):
        rows = rows_of(i)
        u = mm(h2[rows, :], wu_ref[...]) + bu_ref[...]
        g, slope = gelu_both(u)
        gb = g.astype(BF)
        gs[rows, :] = gb
        yacc[rows, :] += mm(gb, wd_ref[...])
        du = (mm(dm[rows, :], wd_ref[...], NT) * slope).astype(BF)
        dus[rows, :] = du
        gbu_ref[...] += jnp.sum(du.astype(F32), 0, keepdims=True)
        dacc[rows, :] += mm(du, wu_ref[...], NT)

    for t in range(FC // 256):
        cols = pl.ds(t * 256, 256)
        gwd_ref[cols, :] = mm(gs[:, cols], dm[...], TN).astype(BF)

    @pl.loop(0, D // 256)
    def _(t):
        rows = pl.ds(pl.multiple_of(t * 256, 256), 256)
        gwu_ref[rows, :] = mm(h2t[rows, :], dus[...]).astype(BF)

    @pl.when(c == FF // FC - 1)
    def _():
        gg2_ref[...] = jnp.zeros_like(gg2_ref)
        gb2_ref[...] = jnp.zeros_like(gb2_ref)
        for row in range(2):
            out_ref[row] = yacc[pl.ds(row * S, SEQ), :].astype(BF)

        @pl.loop(0, T // MB)
        def _(i):
            rows = rows_of(i)
            n2, s2 = norm_parts(x1_ref[rows, :])
            dh = dacc[rows, :]
            gg2_ref[...] += jnp.sum(dh * n2, 0, keepdims=True)
            gb2_ref[...] += jnp.sum(dh, 0, keepdims=True)
            dx1_ref[rows, :] = dm[rows, :].astype(F32) + norm_pull(dh, n2, s2, vec_ref[G2:G2 + 1, :])


def ffn(x1, dm, wide, down, bu, vec):
    one = jax.ShapeDtypeStruct((1, D), F32)
    return pl.pallas_call(
        ffn_kernel,
        grid=(FF // FC,),
        in_specs=[
            whole((T, D)), whole((2, SEQ, D)),
            pl.BlockSpec((D, FC), lambda c: (0, c + UP_AT // FC)), pl.BlockSpec((FC, D), lambda c: (c, 0)),
            pl.BlockSpec((1, FC), lambda c: (0, c)), whole((8, D)),
        ],
        out_specs=[
            whole((2, SEQ, D)), whole((T, D)),
            pl.BlockSpec((D, FC), lambda c: (0, c)), pl.BlockSpec((FC, D), lambda c: (c, 0)),
            pl.BlockSpec((1, FC), lambda c: (0, c)), whole((1, D)), whole((1, D)), whole((1, D)),
        ],
        out_shape=[
            jax.ShapeDtypeStruct((2, SEQ, D), BF), jax.ShapeDtypeStruct((T, D), F32),
            jax.ShapeDtypeStruct((D, FF), BF), jax.ShapeDtypeStruct((FF, D), BF),
            jax.ShapeDtypeStruct((1, FF), F32), one, one, one,
        ],
        scratch_shapes=[
            pltpu.VMEM((T, D), BF), pltpu.VMEM((D, T), BF), pltpu.VMEM((T, D), BF),
            pltpu.VMEM((T, D), F32), pltpu.VMEM((T, D), F32),
            pltpu.VMEM((T, FC), BF), pltpu.VMEM((T, FC), BF),
        ],
        compiler_params=pltpu.CompilerParams(vmem_limit_bytes=LIMIT),
        name="feed_forward",
    )(x1, dm, wide, down, bu, vec)


def attn_bwd_kernel(
    x_ref, dx1_ref, h1_ref, qkv_ref, p_ref, attn_ref, rl_ref, wo_ref, wqkv_ref, vec_ref,
    gx_ref, gwqkv_ref, gwo_ref, gbqkv_ref, gbo_ref, gg1_ref, gb1_ref,
    da, dos, h1t, dqkv,
):
    hq, r = pl.program_id(0), pl.program_id(1)

    @pl.when((hq == 0) & (r == 0))
    def _():
        gbo_ref[...] = jnp.zeros_like(gbo_ref)

        @pl.loop(0, T // MB)
        def _(i):
            rows = rows_of(i)
            d = dx1_ref[rows, :].astype(BF)
            da[rows, :] = d
            gbo_ref[...] += jnp.sum(d.astype(F32), 0, keepdims=True)
            dos[rows, :] = (mm(d, wo_ref[...], NT) * rl_ref[rows, :]).astype(BF)
        h1t[...] = h1_ref[...].T

    rows = pl.ds(pl.multiple_of(r * S, 16), S)
    scale = 1.0 / math.sqrt(HD)
    for j in range(HG // 2):
        at = j * 384
        qp, kp, vp = (qkv_ref[rows, at + 128 * n: at + 128 * (n + 1)] for n in range(3))
        do = dos[rows, pl.ds(pl.multiple_of(hq * QW + j * 128, 128), 128)]
        prod = do.astype(F32) * attn_ref[rows, j * 128:(j + 1) * 128].astype(F32)
        dq = dk = dv = None
        for e in range(2):
            keep = head_lanes((S, 128), e)
            zero = jnp.zeros_like(qp)
            doe = jnp.where(keep, do, zero)
            dot = jnp.sum(jnp.where(keep, prod, 0.0), -1, keepdims=True)
            p = p_ref[0, 2 * j + e]
            ds = (p.astype(F32) * (mm(doe, vp, NT) - dot)).astype(BF)
            a = mm(ds, jnp.where(keep, kp, zero))
            b = mm(ds, jnp.where(keep, qp, zero), TN)
            c = mm(p, doe, TN)
            dq, dk, dv = (a, b, c) if dq is None else (dq + a, dk + b, dv + c)
        for n, part in enumerate((dq * scale, dk * scale, dv)):
            col = hq * GW + j * 384 + n * 128
            dqkv[rows, pl.ds(pl.multiple_of(col, 128), 128)] = part.astype(BF)

    @pl.when(r == 1)
    def _():
        part = dqkv[:, pl.ds(pl.multiple_of(hq * GW, 128), GW)]
        gbqkv_ref[...] = jnp.sum(part.astype(F32), 0, keepdims=True)

        @pl.loop(0, D // 256)
        def _(t):
            rr = pl.ds(pl.multiple_of(t * 256, 256), 256)
            gwqkv_ref[rr, :] = mm(h1t[rr, :], part).astype(BF)
        gwo_ref[...] = mm(attn_ref[...], da[...], TN).astype(BF)

    @pl.when((hq == D // QW - 1) & (r == 1))
    def _():
        gg1_ref[...] = jnp.zeros_like(gg1_ref)
        gb1_ref[...] = jnp.zeros_like(gb1_ref)
        for row in range(2):
            rr = pl.ds(row * S, SEQ)
            dh = mm(dqkv[pl.ds(row * S, S), :], wqkv_ref[...], NT)[:SEQ]
            n1, s1 = norm_parts(x_ref[row].astype(F32))
            gg1_ref[...] += jnp.sum(dh * n1, 0, keepdims=True)
            gb1_ref[...] += jnp.sum(dh, 0, keepdims=True)
            gx_ref[row] = (dx1_ref[rr, :] + norm_pull(dh, n1, s1, vec_ref[G1:G1 + 1, :])).astype(BF)


def attn_bwd(x, dx1, h1, qkv, p, attn, rl, wide, vec):
    act = pl.BlockSpec((T, QW), lambda h, r: (0, h))
    one = jax.ShapeDtypeStruct((1, D), F32)
    return pl.pallas_call(
        attn_bwd_kernel,
        grid=(D // QW, 2),
        in_specs=[
            whole((2, SEQ, D)), whole((T, D)), whole((T, D)), pl.BlockSpec((T, GW), lambda h, r: (0, h)),
            pl.BlockSpec((1, HG, S, S), lambda h, r: (r, h, 0, 0)), act, whole((T, D)),
            pl.BlockSpec((D, D), lambda h, r: (0, 3)), whole((D, 3 * D)), whole((8, D)),
        ],
        out_specs=[
            whole((2, SEQ, D)), pl.BlockSpec((D, GW), lambda h, r: (0, h)),
            pl.BlockSpec((QW, D), lambda h, r: (h, 0)),
            pl.BlockSpec((1, GW), lambda h, r: (0, h)), whole((1, D)), whole((1, D)), whole((1, D)),
        ],
        out_shape=[
            jax.ShapeDtypeStruct((2, SEQ, D), BF), jax.ShapeDtypeStruct((D, 3 * D), BF), jax.ShapeDtypeStruct((D, D), BF),
            jax.ShapeDtypeStruct((1, 3 * D), F32), one, one, one,
        ],
        scratch_shapes=[
            pltpu.VMEM((T, D), BF), pltpu.VMEM((T, D), BF), pltpu.VMEM((D, T), BF), pltpu.VMEM((T, 3 * D), BF),
        ],
        compiler_params=pltpu.CompilerParams(vmem_limit_bytes=LIMIT),
        name="attention_backward",
    )(x, dx1, h1, qkv, p, attn, rl, wide, wide, vec)


NZ = 4
CH = 48
HW = 384
SW = 384


def where_am_i():
    dp, fs = lax.axis_index("dp"), lax.axis_index("fsdp")
    return lax.div(dp, 2), lax.rem(dp, 2), lax.div(fs, 2), lax.rem(fs, 2)


def device(z, x, y, c):
    return (z * 2 + x, y * 2 + c)


def partners(z, x, y, c):
    found = [device(lax.rem(z + k, NZ), x, y, c) for k in (1, 2, 3)]
    return found + [device(z, 1 - x, y, c), device(z, x, 1 - y, c), device(z, x, y, 1 - c)]


def greet(here):
    barrier = pltpu.get_barrier_semaphore()
    others = partners(*here)
    for other in others:
        pl.semaphore_signal(barrier, inc=1, device_id=other, device_id_type=MESH)
    pl.semaphore_wait(barrier, len(others))


def remote(src, dst, sems, n, target):
    return pltpu.make_async_remote_copy(
        src_ref=src, dst_ref=dst, send_sem=sems[0].at[n], recv_sem=sems[1].at[n],
        device_id=target, device_id_type=MESH,
    )


class Gather:
    COPIES = 7

    def __init__(self, here, sems, base, view, other_view, first):
        self.here, self.sems, self.base = here, sems, base
        z, x, y, c = here
        one = lambda i: pl.ds(i, 1)
        every = pl.ds(0, NZ)
        peers = partners(*here)
        mine = view(one(z), one(x), one(y))
        column = view(every, one(x), one(y))
        fx, fy = jnp.where(c == 0, 1 - x, x), jnp.where(c == 0, y, 1 - y)
        tx, ty = jnp.where(c == 0, x, 1 - x), jnp.where(c == 0, 1 - y, y)
        passed = view(every, one(fx), one(fy))
        all_of = view(every, pl.ds(0, 2), pl.ds(0, 2))
        make = lambda n, src, dst, to: remote(src, dst, sems, base + n, to)
        self.along_z = [make(k, first, mine, peers[k]) for k in range(3)]
        self.along_x = make(3, column, column, peers[3])
        self.along_y = make(4, column, column, peers[4])
        self.diagonal = make(5, passed, passed, device(z, tx, ty, c))
        self.sibling = make(6, all_of, all_of, peers[5])

    def start(self, phase):
        if phase == 0:
            for copy in self.along_z:
                copy.start()
        elif phase == 1:
            for copy in self.along_z:
                copy.wait_recv()
            self.along_x.start()
            self.along_y.start()
        elif phase == 2:
            self.along_x.wait_recv()
            self.along_y.wait_recv()
            self.diagonal.start()
        elif phase == 3:
            self.diagonal.wait_recv()
            self.sibling.start()
        else:
            self.sibling.wait_recv()
            for copy in (*self.along_z, self.along_x, self.along_y, self.diagonal, self.sibling):
                copy.wait_send()


N_WIDE = AW // (2 * HW)
N_DOWN = 2
DH = 2 * CH


def gather_kernel(
    wqkv_ref, wout_ref, wup_ref, wdown_ref, small_ref,
    wide_ref, down_ref, vec_ref, bu_ref, bqkv_ref,
    staged, swap, block, smalls, sems_s, sems_r, swap_s, swap_r, own_sem, small_s, small_r,
):
    here = where_am_i()
    z, x, y, c = here
    peers = partners(*here)
    for pair in range(6):
        for n in range(3):
            at = pair * 384 + n * 128
            staged[:, at:at + 128] = wqkv_ref[:, n * D + pair * 128:n * D + (pair + 1) * 128].astype(F32)
    staged[:, OUT_AT:UP_AT] = wout_ref[...].astype(F32)
    staged[:, UP_AT:] = wup_ref[...].astype(F32)
    smalls[z, x, y, c] = small_ref[...]
    greet(here)

    sems = (sems_s, sems_r)

    def half(i, core):
        return pl.ds(pl.multiple_of(i * 2 * HW + core * HW, 128), HW)

    swaps = []
    for i in range(N_WIDE):
        copy = remote(staged.at[:, half(i, 1 - c)], swap.at[:, i * HW:(i + 1) * HW], (swap_s, swap_r), i, peers[5])
        copy.start()
        swaps.append(copy)

    one = lambda i: pl.ds(i, 1)

    def small_at(zs, xs, ys, cs):
        return smalls.at[zs, xs, ys, cs]

    def small_copy(n, src, to):
        return remote(src, src, (small_s, small_r), n, to)

    mine = small_at(one(z), one(x), one(y), one(c))
    both = small_at(one(z), one(x), one(y), pl.ds(0, 2))
    column = small_at(pl.ds(0, NZ), one(x), one(y), pl.ds(0, 2))
    plane = small_at(pl.ds(0, NZ), pl.ds(0, 2), one(y), pl.ds(0, 2))
    small_c = small_copy(0, mine, peers[5])
    small_z = [small_copy(1 + k, both, peers[k]) for k in range(3)]
    small_x = small_copy(4, column, peers[3])
    small_y = small_copy(5, plane, peers[4])
    small_c.start()

    items = []
    own = []
    for i in range(N_DOWN):
        rows = lambda core, i=i: pl.ds(pl.multiple_of(core * DH + i * CH, 16), CH)
        view = lambda zs, xs, ys, rows=rows: down_ref.at[zs, xs, ys, rows(c)]
        first = wdown_ref.at[:, :, :, pl.ds(i * CH, CH)]
        items.append(Gather(here, sems, i * Gather.COPIES, view, None, first))
        own.append(pltpu.make_async_copy(first, view(one(z), one(x), one(y)), own_sem.at[i]))
    for i in range(N_WIDE):
        view = lambda zs, xs, ys, i=i: wide_ref.at[zs, xs, ys, :, half(i, c)]
        first = block.at[:, :, :, :, pl.ds(i * HW, HW)]
        n = N_DOWN + i
        items.append(Gather(here, sems, n * Gather.COPIES, view, None, first))
        own.append(pltpu.make_async_copy(first, view(one(z), one(x), one(y)), own_sem.at[n]))
    order = list(range(N_DOWN, N_DOWN + N_WIDE)) + list(range(N_DOWN))

    small_c.wait_recv()
    for copy in small_z:
        copy.start()
    for i in range(N_WIDE):
        swaps[i].wait_recv()
        mine_part = staged[:, half(i, c)]
        their_part = swap[:, i * HW:(i + 1) * HW]

        @pl.when(c == 0)
        def _(i=i, mine_part=mine_part, their_part=their_part):
            block[0, 0, 0, :, i * HW:(i + 1) * HW] = jnp.concatenate([mine_part, their_part], 0).astype(BF)

        @pl.when(c == 1)
        def _(i=i, mine_part=mine_part, their_part=their_part):
            block[0, 0, 0, :, i * HW:(i + 1) * HW] = jnp.concatenate([their_part, mine_part], 0).astype(BF)
        items[N_DOWN + i].start(0)
        own[N_DOWN + i].start()
    for i in range(N_DOWN):
        items[i].start(0)
        own[i].start()
    for copy in small_z:
        copy.wait_recv()
    small_x.start()
    for n, i in enumerate(order):
        own[i].wait()
        items[i].start(1)
        if n == 1:
            small_x.wait_recv()
            small_y.start()
    for i in order:
        items[i].start(2)
    for i in order:
        items[i].start(3)
    small_y.wait_recv()
    pieces = smalls[...].reshape(32, 8, SW)[:, 0, :].astype(BF)

    def joined(lead, size, width):
        src = lax.broadcasted_iota(jnp.int32, (SW, size), 0)
        dst = lax.broadcasted_iota(jnp.int32, (SW, size), 1)
        spread = jnp.where(src == lead + lax.rem(dst, width), 1.0, 0.0).astype(BF)
        dev = lax.broadcasted_iota(jnp.int32, (32, size), 0)
        col = lax.broadcasted_iota(jnp.int32, (32, size), 1)
        return jnp.sum(jnp.where(lax.div(col, width) == dev, mm(pieces, spread), 0.0), 0, keepdims=True)

    rows = [joined(24 * i, D, 24) for i in range(8)]
    for i in range(8):
        vec_ref[i:i + 1, :] = rows[i]
    bu_ref[...] = joined(192, FF, 96)
    for pair in range(6):
        at = pair * 384
        bqkv_ref[:, at:at + 128] = rows[BQ][:, pair * 128:(pair + 1) * 128]
        bqkv_ref[:, at + 128:at + 256] = jnp.zeros((1, 128), F32)
        bqkv_ref[:, at + 256:at + 384] = rows[BV][:, pair * 128:(pair + 1) * 128]
    for i in order:
        items[i].start(4)
    for copy in (*swaps, small_c, *small_z, small_x, small_y):
        copy.wait_send()


def gather(wqkv, wout, wup, wdown, small):
    n = N_WIDE + N_DOWN
    vm = lambda: pl.BlockSpec(memory_space=pltpu.VMEM)
    hbm = lambda: pl.BlockSpec(memory_space=pl.ANY)
    sem = lambda k: pltpu.SemaphoreType.DMA((k,))
    return pl.pallas_call(
        gather_kernel,
        in_specs=[vm()] * 5,
        out_specs=[hbm(), hbm(), vm(), vm(), vm()],
        out_shape=[
            jax.ShapeDtypeStruct((NZ, 2, 2, CH, AW), BF), jax.ShapeDtypeStruct((NZ, 2, 2, 4 * CH, D), BF),
            jax.ShapeDtypeStruct((8, D), F32), jax.ShapeDtypeStruct((1, FF), F32), jax.ShapeDtypeStruct((1, 3 * D), F32),
        ],
        scratch_shapes=[
            pltpu.VMEM((CH // 2, AW), F32), pltpu.VMEM((CH // 2, AW // 2), F32), pltpu.VMEM((1, 1, 1, CH, AW // 2), BF),
            pltpu.VMEM((NZ, 2, 2, 2, 8, SW), F32),
            sem(n * Gather.COPIES), sem(n * Gather.COPIES), sem(N_WIDE), sem(N_WIDE), sem(n), sem(6), sem(6),
        ],
        compiler_params=pltpu.CompilerParams(collective_id=0, has_side_effects=True, vmem_limit_bytes=LIMIT),
        name="gather_parameters",
    )(wqkv, wout, wup, wdown.reshape(1, 1, 1, 4 * CH // 2, D), small)


class Scatter:
    COPIES = 7

    def __init__(self, here, sems, base, theirs, mine, acc, via, last, zs):
        self.mine, self.acc, self.via, self.last, self.zs = mine, acc, via, last, zs
        z, x, y, c = here
        self.here = here
        peers = partners(*here)
        one = lambda i: pl.ds(i, 1)
        every = pl.ds(0, NZ)
        ix, iy = jnp.where(c == 0, x, 1 - x), jnp.where(c == 0, 1 - y, y)
        self.px, self.py = jnp.where(c == 0, 1 - x, x), jnp.where(c == 0, y, 1 - y)
        first, second = device(z, ix, iy, c), device(z, self.px, self.py, c)
        make = lambda n, src, dst, to: remote(src, dst, sems, base + n, to)
        at = lambda xs, ys: acc.at[every, one(xs), one(ys)]
        self.swap = make(0, theirs, acc, peers[5])
        self.far = make(1, at(1 - x, 1 - y), via.at[0], first)
        self.near = make(2, at(ix, iy), via.at[1], first)
        self.next = make(3, at(self.px, self.py), last, second)
        self.along_z = [
            make(4 + k, acc.at[one(lax.rem(z + k + 1, NZ)), one(x), one(y)], zs.at[k], peers[k]) for k in range(3)
        ]

    def start(self, phase):
        z, x, y, c = self.here
        acc = self.acc
        one = lambda i: pl.ds(i, 1)
        every = pl.ds(0, NZ)
        f = lambda v: v.astype(F32)
        if phase == 0:
            self.swap.start()
        elif phase == 1:
            self.swap.wait_recv()

            @pl.loop(0, NZ)
            def _(i):
                for xi in range(2):
                    for yi in range(2):
                        acc[i, xi, yi] = (f(acc[i, xi, yi]) + f(self.mine(i, xi, yi))).astype(BF)
            self.far.start()
            self.near.start()
        elif phase == 2:
            self.far.wait_recv()
            px, py = self.px, self.py

            @pl.loop(0, NZ)
            def _(i):
                acc[i, px, py] = (f(acc[i, px, py]) + f(self.via[0, i, 0, 0])).astype(BF)
            self.next.start()
            self.near.wait_recv()

            @pl.loop(0, NZ)
            def _(i):
                acc[i, x, y] = (f(acc[i, x, y]) + f(self.via[1, i, 0, 0])).astype(BF)
        elif phase == 3:
            self.next.wait_recv()

            @pl.loop(0, NZ)
            def _(i):
                acc[i, x, y] = (f(acc[i, x, y]) + f(self.last[i, 0, 0])).astype(BF)
            for copy in self.along_z:
                copy.start()
        else:
            for copy in self.along_z:
                copy.wait_recv()
            for copy in (self.swap, self.far, self.near, self.next, *self.along_z):
                copy.wait_send()
            return f(acc[z, x, y]) + f(self.zs[0, 0, 0, 0]) + f(self.zs[1, 0, 0, 0]) + f(self.zs[2, 0, 0, 0])


N_QKV = 3
N_UP = FF // D


def scatter_kernel(
    gqkv_ref, gout_ref, gup_ref, gdown_ref, small_ref,
    oqkv_ref, oout_ref, oup_ref, odown_ref, osmall_ref, obu_ref,
    acc_w, via_w, last_w, zs_w, acc_d, via_d, last_d, zs_d, done, small_in,
    sems_s, sems_r, fin_s, fin_r, small_s, small_r,
):
    here = where_am_i()
    z, x, y, c = here
    peers = partners(*here)
    greet(here)
    sems = (sems_s, sems_r)

    def half(i, core):
        return pl.ds(pl.multiple_of(i * 2 * HW + core * HW, 128), HW)

    items = []
    every = pl.ds(0, NZ)
    two = pl.ds(0, 2)
    for i in range(N_DOWN):
        rows = lambda core, i=i: pl.ds(pl.multiple_of(core * DH + i * CH, 16), CH)
        theirs = gdown_ref.at[every, two, two, rows(1 - c)]
        mine = lambda a, b, d, rows=rows: gdown_ref[a, b, d, rows(c)]
        items.append(Scatter(here, sems, i * 7, theirs, mine, acc_d.at[i], via_d.at[i], last_d.at[i], zs_d.at[i]))
    wide = [(gup_ref, i) for i in range(N_UP)] + [(gout_ref, 0)] + [(gqkv_ref, i) for i in range(N_QKV)]
    for n, (ref, i) in enumerate(wide):
        theirs = ref.at[every, two, two, :, half(i, 1 - c)]
        mine = lambda a, b, d, ref=ref, i=i: ref[a, b, d, :, half(i, c)]
        items.append(
            Scatter(here, sems, (N_DOWN + n) * 7, theirs, mine, acc_w.at[n], via_w.at[n], last_w.at[n], zs_w.at[n])
        )
    small_in[0] = small_ref[...]
    small_copies = []

    def small_step(n, src, dst, to):
        copy = remote(small_in.at[src], small_in.at[dst], (small_s, small_r), n, to)
        copy.start()
        small_copies.append(copy)
        return copy

    small_step(0, 0, 1, peers[5])
    for item in items:
        item.start(0)
    small_copies[0].wait_recv()
    small_in[2] = small_in[0] + small_in[1]
    small_step(1, 2, 3, peers[3])
    for item in items:
        item.start(1)
    small_copies[1].wait_recv()
    small_in[4] = small_in[2] + small_in[3]
    small_step(2, 4, 5, peers[4])
    for item in items:
        item.start(2)
    small_copies[2].wait_recv()
    small_in[6] = small_in[4] + small_in[5]
    for k in range(3):
        small_step(3 + k, 6, 7 + k, peers[k])
    for item in items:
        item.start(3)
    for k in range(3):
        small_copies[3 + k].wait_recv()
    total = small_in[6] + small_in[7] + small_in[8] + small_in[9]
    me = lax.axis_index("dp") * lax.axis_size("fsdp") + lax.axis_index("fsdp")
    src = lax.broadcasted_iota(jnp.int32, (D, 128), 0)
    dst = lax.broadcasted_iota(jnp.int32, (D, 128), 1)

    def pick(rows, width, at):
        chosen = jnp.where((src == at + dst) & (dst < width), 1.0, 0.0)
        return lax.dot_general(rows, chosen, NN, precision=lax.Precision.HIGHEST, preferred_element_type=F32)

    osmall_ref[...] = pick(total[:8], 24, me * 24)
    row = lax.broadcasted_iota(jnp.int32, (8, D), 0)
    longest = jnp.sum(jnp.where(row == lax.div(me, 8), total[8:16], 0.0), 0, keepdims=True)
    obu_ref[...] = pick(jnp.broadcast_to(longest, (8, D)), 96, lax.rem(me, 8) * 96)
    for i in range(N_DOWN):
        odown_ref[pl.ds(i * CH, CH), :] = items[i].start(4)
    finals = []
    for n, (ref, i) in enumerate(wide):
        done[n] = items[N_DOWN + n].start(4)
        mine = done.at[n, pl.ds(pl.multiple_of(c * 24, 8), 24)]
        other = done.at[n, pl.ds(pl.multiple_of((1 - c) * 24, 8), 24)]
        if ref is gqkv_ref:
            for b in range(3):
                cols = pl.ds(pl.multiple_of(b * D + i * QW + c * 128, 128), 128)
                k = N_UP + 1 + i * 3 + b
                part = pl.ds(b * 128, 128)
                copy = remote(
                    done.at[n, pl.ds(pl.multiple_of((1 - c) * 24, 8), 24), part], oqkv_ref.at[:, cols],
                    (fin_s, fin_r), k, peers[5],
                )
                copy.start()
                finals.append(copy)
                oqkv_ref[:, cols] = done[n, pl.ds(pl.multiple_of(c * 24, 8), 24), part]
        else:
            target = oout_ref if ref is gout_ref else oup_ref
            copy = remote(other, target.at[:, half(i, c)], (fin_s, fin_r), n, peers[5])
            copy.start()
            finals.append(copy)
            target[:, half(i, c)] = mine[...]
    for copy in finals:
        copy.wait()
    for copy in small_copies:
        copy.wait_send()


def scatter(gqkv, gout, gup, gdown, small):
    nw = N_QKV + 1 + N_UP
    vm = lambda: pl.BlockSpec(memory_space=pltpu.VMEM)
    sem = lambda k: pltpu.SemaphoreType.DMA((k,))
    chips = lambda v: v.reshape(NZ, 2, 2, v.shape[0] // 16, v.shape[1])
    n = (nw + N_DOWN) * 7
    return pl.pallas_call(
        scatter_kernel,
        in_specs=[vm()] * 5,
        out_specs=[vm()] * 6,
        out_shape=[
            jax.ShapeDtypeStruct((24, 3 * D), F32), jax.ShapeDtypeStruct((24, D), F32),
            jax.ShapeDtypeStruct((24, FF), F32), jax.ShapeDtypeStruct((96, D), F32),
            jax.ShapeDtypeStruct((8, 128), F32), jax.ShapeDtypeStruct((8, 128), F32),
        ],
        scratch_shapes=[
            pltpu.VMEM((nw, NZ, 2, 2, CH, HW), BF), pltpu.VMEM((nw, 2, NZ, 1, 1, CH, HW), BF),
            pltpu.VMEM((nw, NZ, 1, 1, CH, HW), BF), pltpu.VMEM((nw, 3, 1, 1, 1, CH, HW), BF),
            pltpu.VMEM((N_DOWN, NZ, 2, 2, CH, D), BF), pltpu.VMEM((N_DOWN, 2, NZ, 1, 1, CH, D), BF),
            pltpu.VMEM((N_DOWN, NZ, 1, 1, CH, D), BF), pltpu.VMEM((N_DOWN, 3, 1, 1, 1, CH, D), BF),
            pltpu.VMEM((nw, CH, HW), F32), pltpu.VMEM((10, 16, D), F32),
            sem(n), sem(n), sem(N_UP + 1 + 9), sem(N_UP + 1 + 9), sem(6), sem(6),
        ],
        compiler_params=pltpu.CompilerParams(collective_id=1, has_side_effects=True, vmem_limit_bytes=LIMIT),
        name="sum_gradients",
    )(chips(gqkv), chips(gout), chips(gup), chips(gdown), small)


def by_pair(v):
    return v.reshape(v.shape[0], 3, 6, 128).transpose(0, 2, 1, 3).reshape(v.shape[0], 3 * D)


def by_kind(v):
    return v.reshape(v.shape[0], 6, 3, 128).transpose(0, 2, 1, 3).reshape(v.shape[0], 3 * D)


def on_device(copies, inputs, row_kind, ln1_gain, ln1_bias, w_qkv, b_query, b_value, w_out, b_out, ln2_gain, ln2_bias, w_up, b_up, w_down, b_down, out_grad):
    axes = ("dp", "fsdp")
    vectors = (ln1_gain, ln1_bias, b_query, b_value, b_out, ln2_gain, ln2_bias, b_down)
    if copies:
        small = jnp.concatenate([*vectors, b_up]).astype(F32)
        small = jnp.broadcast_to(jnp.pad(small, (0, SW - small.shape[0]))[None], (8, SW))
        wide, down, vec, bu, bqkv = gather(w_qkv, w_out, w_up, w_down, small)
        wide, down = wide.reshape(D, AW), down.reshape(FF, D)
    else:
        get = lambda v: lax.all_gather(v, axes, axis=0, tiled=True)
        wide = jnp.concatenate([by_pair(get(w_qkv)), get(w_out), get(w_up)], 1)
        down = get(w_down)
        full = [get(v).astype(F32) for v in vectors]
        vec = jnp.stack(full)
        bu = get(b_up).astype(F32)[None]
        bqkv = by_pair(jnp.concatenate([full[BQ], jnp.zeros_like(full[BQ]), full[BV]])[None])
    h1, qkv, p, attn, rl, x1 = attn_fwd(row_kind, inputs, wide, bqkv, vec)
    outputs, dx1, gup, gdown, gbu, gg2, gb2, gbd = ffn(x1, out_grad, wide, down, bu, vec)
    input_grad, gqkv, gout, gbqkv, gbo, gg1, gb1 = attn_bwd(inputs, dx1, h1, qkv, p, attn, rl, wide, vec)
    gbqkv = by_kind(gbqkv)
    small = [gg1, gb1, gbqkv[:, :D], gbqkv[:, 2 * D:], gbo, gg2, gb2, gbd]
    if copies:
        small = jnp.concatenate([*small, gbu.reshape(4, D), jnp.zeros((4, D), F32)], 0)
        gqkv, gout, gup, gdown, small, gbu = scatter(gqkv, gout, gup, gdown, small)
        small = [small[i, :24] for i in range(8)]
        gbu = gbu[0, :96]
    else:
        give = lambda v: lax.psum_scatter(v.astype(F32), axes, scatter_dimension=0, tiled=True)
        gqkv, gout, gup, gdown = give(by_kind(gqkv)), give(gout), give(gup), give(gdown)
        small = [give(v[0]) for v in small]
        gbu = give(gbu[0])
    gg1, gb1, gbq, gbv, gbo, gg2, gb2, gbd = small
    return outputs, input_grad, gg1, gb1, gqkv, gbq, gbv, gout, gbo, gg2, gb2, gup, gbu, gdown, gbd


def solution(mesh):
    both = ("dp", "fsdp")
    row = P(both)
    mat = P(both, None)
    act = P(both, None, None)
    in_specs = (act, row, row, row, mat, row, row, mat, row, row, row, mat, row, mat, row, act)
    out_specs = (act, act, row, row, mat, row, row, mat, row, row, row, mat, row, mat, row)
    copies = mesh.shape["dp"] == 2 * NZ and mesh.shape["fsdp"] == 4
    return jax.shard_map(
        functools.partial(on_device, copies), mesh=mesh, in_specs=in_specs, out_specs=out_specs, check_vma=False
    )
```

time: 859 us -> 377 us (0.44)
  Pallas kernels: 0 us -> 351 us
  waiting for transfers between devices: 325 us -> 0 us
  matrix products: 241 us -> 0 us
  local copies, waits for them, and re-layouts: 113 us -> 23.7 us
  blocking collectives: 84.5 us -> 0 us
  other arithmetic: 72.8 us -> 1.41 us
  between operations: 15.1 us -> 0.81 us
    pallas_call x0 -> x5, Pallas kernels: none -> 351 us  [the longest x1 116 us: scatter(): pl.pallas_call(scatter_kernel, in_specs=[vm()] * 5, out_specs=[vm()] * 6,...]
    reduce_scatter x4 -> x0, waiting for transfers between devices: 292 us -> none  [the longest x1 142 us: on_device(): lax.psum_scatter(grad_w_down, ('dp', 'fsdp'), scatter_dimension=0, tiled=...]
    dot_general x18 -> x0, matrix products: 241 us -> none  [the longest x1 38 us: feedforward_forward(): jnp.dot(normed_mid, w_up, preferred_element_type=jnp.float32)]
    unnamed x2 -> x0, blocking collectives: 84.5 us -> none
    convert_element_type x13 -> x0, other arithmetic: 38.9 us -> none  [the longest x1 27.8 us: attention_back(): (attention_probs * (grad_probs - row_dot)).astype(jnp.bfloat16)]
    reshape x7 -> x3, local copies, waits for them, and re-layouts: 37.5 us -> 0.04 us  [the longest x2 0.03 us: by_kind(): v.reshape(v.shape[0], 6, 3, 128).transpose(0, 2, 1, 3)]
    reduce_sum x7 -> x0, other arithmetic: 33.3 us -> none  [the longest x1 14.5 us: attention_forward(): jnp.sum(jnp.exp(scores - row_max), -1, keepdims=True)]
    all_gather x4 -> x0, waiting for transfers between devices: 31 us -> none  [the longest x1 27.2 us: on_device(): lax.all_gather(w_down, ('dp', 'fsdp'), axis=0, tiled=True)]
  transfers between devices with their start and end apart: 8 -> 0, of which waited for: 5 -> 0; matrix products, arithmetic and copies ran while one was open for 46% -> 0% of each run, Pallas kernels for 0% -> 0%
where the time goes in v1:
time: 377 us
  Pallas kernels  351 us (93%)
  local copies, waits for them, and re-layouts  23.7 us (6%)
    pallas_call x1, Pallas kernels, scatter(): pl.pallas_call(scatter_kernel, in_specs=[vm()] * 5, out_specs=[vm()] * 6,...  116 us
    pallas_call x1, Pallas kernels, gather(): pl.pallas_call(gather_kernel, in_specs=[vm()] * 5, out_specs=[hbm(), hbm(...  87.7 us
    pallas_call x1, Pallas kernels, ffn(): pl.pallas_call(ffn_kernel, grid=(FF // FC,), in_specs=[whole((T, D)), who...  65 us
    pallas_call x1, Pallas kernels, attn_bwd(): pl.pallas_call(attn_bwd_kernel, grid=(D // QW, 2), in_specs=[whole((2, SE...  48 us
    pallas_call x1, Pallas kernels, attn_fwd(): pl.pallas_call(attn_fwd_kernel, grid=(D // QW, 2), in_specs=[pl.BlockSpec...  34.5 us
    unnamed x30, local copies, waits for them, and re-layouts  11.8 us

profile of v1, /device:TPU:0, one launch (start us, length us, event | category | flops | bytes accessed | tf_op | source)
XLA Modules:
  0.0 376.6 jit_solution(16920730662303015739)
XLA Ops:
  0.6 6.1 %concatenate.6 = bf16[288]{0:T(512)(128)(2,1)S(1)} concatenate(bf16[24]{0:T(256)(128)(2,1)} %param.18, bf16[24]{0:T(256)(128)(2,1)} %param.19, bf16[24]{0:T(256)(128)(2,1)} %param.21, bf16[24]{0:T(256)(128)(2,1)} %param.22, bf16[24]{0:T(256)(128)(2,1)} %param.24, bf16[24]{0:T(256)(128)(2,1)} %param.25, bf16[24]{0:T(256)(128)(2,1)} %param.26, bf16[24]{0:T(256)(128)(2,1)} %param.30, ...), dimensions={0} | concatenate | bytes 1152 | tf_op jit(solution)/shard_map/concatenate | solution.py:811
  6.8 0.6 broadcast_in_dim.4.small_ref
  7.4 87.7 %gather_parameters.1 = (bf16[4,2,2,48,6144]{4,3,2,1,0:T(8,128)(2,1)}, bf16[4,2,2,192,768]{4,3,2,1,0:T(8,128)(2,1)}, f32[8,768]{1,0:T(8,128)}, f32[1,3072]{1,0:T(1,128)}, f32[1,2304]{1,0:T(1,128)}) custom-call(bf16[24,2304]{1,0:T(8,128)(2,1)} %wqkv_ref.1, bf16[24,768]{1,0:T(8,128)(2,1)} %wout_ref.1, bf16[24,3072]{1,0:T(8,128)(2,1)} %wup_ref.1, ...), custom_call_target="tpu_custom_call" | custom-call | tf_op jit(solution)/shard_map/gather_parameters/pallas_call | solution.py:575
  95.1 2.8 copy.37.x_ref
  97.8 0.0 copy-start.2
  97.8 34.5 %attention_forward.1 = (bf16[1088,768]{1,0:T(8,128)(2,1)}, bf16[1088,2304]{1,0:T(8,128)(2,1)}, bf16[2,12,544,544]{3,2,1,0:T(8,128)(2,1)}, bf16[1088,768]{1,0:T(8...) custom-call(s32[2]{0:T(128)} %kind_ref.1, bf16[2,529,768]{2,1,0:T(8,128)(2,1)} %copy.37.x_ref, ...), custom_call_target="tpu_custom_call" | custom-call | tf_op jit(solution)/shard_map/attention_forward/pallas_call | solution.py:151
  132.3 0.0 copy-done.2
  132.3 1.4 copy.38.dm_ref
  133.7 65.0 %feed_forward.1 = (bf16[2,529,768]{2,1,0:T(8,128)(2,1)}, f32[1088,768]{1,0:T(8,128)}, bf16[768,3072]{1,0:T(8,128)(2,1)}, bf16[3072,768]{1,0:T(8,128)(2,1)}, f32[...) custom-call(f32[1088,768]{1,0:T(8,128)} %get-tuple-element.50.x1_ref, ...), custom_call_target="tpu_custom_call" | custom-call | tf_op jit(solution)/shard_map/feed_forward/pallas_call | solution.py:242
  198.7 0.0 copy-start.7
  198.7 0.0 copy-start.8
  198.7 0.0 copy-start.9
  198.7 0.0 copy-start.10
  198.8 48.0 %attention_backward.1 = (bf16[2,529,768]{2,1,0:T(8,128)(2,1)}, bf16[768,2304]{1,0:T(8,128)(2,1)}, bf16[768,768]{1,0:T(8,128)(2,1)}, f32[1,2304]{1,0:T(1,128)}, f...) custom-call(bf16[2,529,768]{2,1,0:T(8,128)(2,1)} %copy.37.x_ref, f32[1088,768]{1,0:T(8,128)} %get-tuple-element.54.dx1_ref, ...), custom_call_target="tpu_custom_call" | custom-call | tf_op jit(solution)/shard_map/attention_backward/pallas_call | solution.py:340
  246.7 0.7 reduce
  247.5 0.5 broadcast.7
  248.0 0.0 copy-done.7
  248.0 0.7 reduce.4
  248.7 0.0 copy-done.8
  248.7 0.0 copy-done.9
  248.8 0.0 copy-done.10
  248.8 2.0 concatenate.7.small_ref
  250.7 0.0 copy-start.1
  250.7 115.5 %sum_gradients.1 = (f32[24,2304]{1,0:T(8,128)}, f32[24,768]{1,0:T(8,128)}, f32[24,3072]{1,0:T(8,128)}, f32[96,768]{1,0:T(8,128)}, f32[8,128]{1,0:T(8,128)}, /*index=5*/f32[8,128]{1,0:T(8,128)}) custom-call(bf16[4,2,2,48,2304]{4,3,2,1,0:T(8,128)(2,1)} %bitcast.34, bf16[4,2,2,48,768]{4,3,2,1,0:T(8,128)(2,1)} %bitcast.35, ...), custom_call_target="tpu_custom_call" | custom-call | tf_op jit(solution)/shard_map/sum_gradients/pallas_call | solution.py:777
  366.2 0.0 copy-start
  366.2 1.5 slice_bitcast_fusion
  367.8 1.2 slice_bitcast_fusion.1
  369.0 0.0 copy-done.1
  369.0 2.4 copy.42
  371.4 0.0 copy-start.5
  371.4 0.0 copy-done
  371.4 0.0 copy-start.6
  371.4 0.0 copy-start.4
  371.4 0.0 copy-start.3
  371.4 2.4 copy.41
  373.8 0.0 copy-done.5
  373.8 0.7 copy.47
  374.5 0.0 copy-done.6
  374.5 0.6 copy.48
  375.1 0.0 copy-done.4
  375.1 0.7 copy.49
  375.9 0.0 copy-done.3
  375.9 0.7 copy.50
  (7 shorter events, 0.1 us)
Async XLA Ops:
  97.8 34.5 %copy-start.2 = (bf16[2,529,768]{2,0,1:T(2,128)(2,1)S(1)}, bf16[2,529,768]{2,0,1:T(2,128)(2,1)}, u32[]{:S(2)}) copy-start(bf16[2,529,768]{2,0,1:T(2,128)(2,1)} %param.31) | copy-start | bytes 4875268
  198.7 49.3 %copy-start.7 = (f32[1,3072]{1,0:T(1,128)S(1)}, f32[1,3072]{1,0:T(1,128)}, u32[]{:S(2)}) copy-start(f32[1,3072]{1,0:T(1,128)} %get-tuple-element.72) | copy-start | bytes 36868
  198.7 50.0 %copy-start.8 = (f32[1,768]{1,0:T(1,128)S(1)}, f32[1,768]{1,0:T(1,128)}, u32[]{:S(2)}) copy-start(f32[1,768]{1,0:T(1,128)} %get-tuple-element.69) | copy-start | bytes 9220
  198.7 50.0 %copy-start.9 = (f32[1,768]{1,0:T(1,128)S(1)}, f32[1,768]{1,0:T(1,128)}, u32[]{:S(2)}) copy-start(f32[1,768]{1,0:T(1,128)} %get-tuple-element.70) | copy-start | bytes 9220
  198.7 50.0 %copy-start.10 = (f32[1,768]{1,0:T(1,128)S(1)}, f32[1,768]{1,0:T(1,128)}, u32[]{:S(2)}) copy-start(f32[1,768]{1,0:T(1,128)} %get-tuple-element.71) | copy-start | bytes 9220
  250.7 118.2 %copy-start.1 = (bf16[2,529,768]{2,1,0:T(8,128)(2,1)S(1)}, bf16[2,529,768]{2,1,0:T(8,128)(2,1)}, u32[]{:S(2)}) copy-start(bf16[2,529,768]{2,1,0:T(8,128)(2,1)} %get-tuple-element.95) | copy-start | bytes 4875268
  366.2 5.1 %copy-start = (bf16[2,529,768]{2,1,0:T(8,128)(2,1)S(1)}, bf16[2,529,768]{2,1,0:T(8,128)(2,1)}, u32[]{:S(2)}) copy-start(bf16[2,529,768]{2,1,0:T(8,128)(2,1)} %get-tuple-element.94) | copy-start | bytes 4875268
  371.4 2.4 copy-start.5
  371.4 3.1 copy-start.6
  371.4 3.8 copy-start.4
  371.4 4.5 %copy-start.3 = (f32[96,768]{1,0:T(8,128)S(1)}, f32[96,768]{1,0:T(8,128)}, u32[]{:S(2)}) copy-start(f32[96,768]{1,0:T(8,128)} %get-tuple-element.147) | copy-start | bytes 884740

commit v2 on v1

v2 whole, which is shorter than its diff:
```python
import functools
import math

import jax
import jax.numpy as jnp
from jax import lax
from jax.experimental import pallas as pl
from jax.experimental.pallas import tpu as pltpu
from jax.sharding import PartitionSpec as P

D = 768
HD = 64
FF = 3072
SEQ = 529
HALF = 264
EPS = 1e-06
S = 544
T = 2 * S
MB = 272
HG = 4
QW = HG * HD
GW = 3 * QW
FC = 512
OUT_AT = 3 * D
UP_AT = 4 * D
AW = 4 * D + FF
F32 = jnp.float32
BF = jnp.bfloat16
LIMIT = 62 * 2**20
MESH = pl.DeviceIdType.MESH
NN = (((1,), (0,)), ((), ()))
NT = (((1,), (1,)), ((), ()))
TN = (((0,), (0,)), ((), ()))


def mm(a, b, dims=NN):
    return lax.dot_general(a, b, dims, preferred_element_type=F32)


def norm_parts(values):
    mean = jnp.mean(values, -1, keepdims=True)
    centred = values - mean
    inverse = lax.rsqrt(jnp.mean(centred * centred, -1, keepdims=True) + EPS)
    return centred * inverse, inverse


def norm_pull(grad, normed, inverse, gain):
    scaled = grad * gain
    return inverse * (
        scaled
        - jnp.mean(scaled, -1, keepdims=True)
        - normed * jnp.mean(scaled * normed, -1, keepdims=True)
    )


def gelu_both(u):
    a = jnp.abs(u)
    t = 1.0 / (1.0 + (0.3275911 / math.sqrt(2.0)) * a)
    e = jnp.exp(-0.5 * u * u)
    poly = t * (
        0.254829592
        + t * (-0.284496736 + t * (1.421413741 + t * (-1.453152027 + t * 1.061405429)))
    )
    tail = 0.5 * poly * e
    phi = jnp.where(u < 0, tail, 1.0 - tail)
    return u * phi, phi + u * e * (1.0 / math.sqrt(2.0 * math.pi))


def head_lanes(shape, e):
    lane = lax.broadcasted_iota(jnp.int32, shape, 1)
    return (lane // HD) == e


def whole(shape):
    return pl.BlockSpec(shape, lambda *_: (0,) * len(shape))


def rows_of(i):
    return pl.ds(pl.multiple_of(i * MB, 16), MB)


G1, B1, BQ, BV, BO, G2, B2, BD = range(8)


def attn_fwd_kernel(
    kind_ref, x_ref, wg_ref, bqkv_ref, wo_ref, vec_ref,
    h1_ref, qkv_ref, p_ref, attn_ref, rl_ref, x1_ref, fa, fb,
):
    hq, r = pl.program_id(0), pl.program_id(1)

    @pl.when((hq == 0) & (r == 0))
    def _():
        for row in range(2):
            h1_ref[pl.ds(row * S + S - 16, 16), :] = jnp.zeros((16, D), BF)
            n1, _s = norm_parts(x_ref[row].astype(F32))
            h1_ref[pl.ds(row * S, SEQ), :] = (n1 * vec_ref[G1:G1 + 1, :] + vec_ref[B1:B1 + 1, :]).astype(BF)
            slot = lax.broadcasted_iota(jnp.int32, (S, 128), 0)
            lane = lax.broadcasted_iota(jnp.int32, (S, 128), 1)
            packed = jnp.where(slot < HALF, 0, jnp.where(slot < 2 * HALF, 1, 2))
            seg = jnp.where(kind_ref[row] == 1, packed, 0)
            fa[row] = jnp.where((lane < 3) & (seg == lane), -1e30, 0.0).astype(BF)
            fb[row] = jnp.where((lane < 3) & ((seg != lane) | (slot >= SEQ)), 1.0, 0.0).astype(BF)

    @pl.when(r == 0)
    def _():
        @pl.loop(0, T // MB)
        def _(i):
            rows = rows_of(i)
            qkv_ref[rows, :] = (mm(h1_ref[rows, :], wg_ref[...]) + bqkv_ref[...]).astype(BF)

    rows = pl.ds(pl.multiple_of(r * S, 16), S)
    feat_q, feat_k = fa[r], fb[r]
    ones = jnp.ones((S, 128), BF)
    scale = math.log2(math.e) / math.sqrt(HD)
    for j in range(HG // 2):
        at = j * 384
        qp, kp, vp = (qkv_ref[rows, at + 128 * n: at + 128 * (n + 1)] for n in range(3))
        kcat = jnp.concatenate([kp, feat_k], 1)
        total = None
        inv = None
        for e in range(2):
            keep = head_lanes((S, 128), e)
            qcat = jnp.concatenate([jnp.where(keep, qp, jnp.zeros_like(qp)), feat_q], 1)
            s = mm(qcat, kcat, NT)
            m = jnp.max(s, -1, keepdims=True)
            pb = jnp.exp2((s - m) * scale).astype(BF)
            p_ref[0, 2 * j + e] = pb
            vcat = jnp.concatenate([jnp.where(keep, vp, jnp.zeros_like(vp)), ones], 1)
            o = mm(pb, vcat)
            rl = 1.0 / o[:, 128:]
            part = o[:, :128] * rl
            total = part if total is None else total + part
            inv = rl if inv is None else jnp.where(keep, rl, inv)
        out = pl.ds(pl.multiple_of(hq * QW + j * 128, 128), 128)
        attn_ref[rows, out] = total.astype(BF)
        rl_ref[rows, out] = inv

    @pl.when((hq == D // QW - 1) & (r == 1))
    def _():
        for row in range(2):
            x1_ref[pl.ds(row * S + S - 16, 16), :] = jnp.zeros((16, D), F32)
            x1_ref[pl.ds(row * S, SEQ), :] = x_ref[row].astype(F32)

        @pl.loop(0, T // MB)
        def _(i):
            rr = rows_of(i)
            x1_ref[rr, :] = x1_ref[rr, :] + mm(attn_ref[rr, :], wo_ref[...]) + vec_ref[BO:BO + 1, :]


def attn_fwd(kind, x, wide, bqkv, vec):
    return pl.pallas_call(
        attn_fwd_kernel,
        grid=(D // QW, 2),
        in_specs=[
            pl.BlockSpec(memory_space=pltpu.SMEM), whole((2, SEQ, D)),
            pl.BlockSpec((D, GW), lambda h, r: (0, h)), pl.BlockSpec((1, GW), lambda h, r: (0, h)),
            pl.BlockSpec((D, D), lambda h, r: (0, 3)), whole((8, D)),
        ],
        out_specs=[
            whole((T, D)), pl.BlockSpec((T, GW), lambda h, r: (0, h)),
            pl.BlockSpec((1, HG, S, S), lambda h, r: (r, h, 0, 0)),
            whole((T, D)), whole((T, D)), whole((T, D)),
        ],
        out_shape=[
            jax.ShapeDtypeStruct((T, D), BF), jax.ShapeDtypeStruct((T, 3 * D), BF),
            jax.ShapeDtypeStruct((2, D // HD, S, S), BF),
            jax.ShapeDtypeStruct((T, D), BF), jax.ShapeDtypeStruct((T, D), F32), jax.ShapeDtypeStruct((T, D), F32),
        ],
        scratch_shapes=[pltpu.VMEM((2, S, 128), BF), pltpu.VMEM((2, S, 128), BF)],
        compiler_params=pltpu.CompilerParams(vmem_limit_bytes=LIMIT),
        name="attention_forward",
    )(kind, x, wide, bqkv, wide, vec)


def ffn_kernel(
    x1_ref, dm_ref, wu_ref, wd_ref, bu_ref, vec_ref,
    out_ref, dx1_ref, gwu_ref, gwd_ref, gbu_ref, gg2_ref, gb2_ref, gbd_ref,
    h2, h2t, dm, yacc, dacc, gs, dus,
):
    c = pl.program_id(0)

    @pl.when(c == 0)
    def _():
        for row in range(2):
            dm[pl.ds(row * S + S - 16, 16), :] = jnp.zeros((16, D), BF)
            dm[pl.ds(row * S, SEQ), :] = dm_ref[row]

        @pl.loop(0, T // MB)
        def _(i):
            rows = rows_of(i)
            x1 = x1_ref[rows, :]
            n2, _s = norm_parts(x1)
            h2[rows, :] = (n2 * vec_ref[G2:G2 + 1, :] + vec_ref[B2:B2 + 1, :]).astype(BF)
            yacc[rows, :] = x1 + vec_ref[BD:BD + 1, :]
            dacc[rows, :] = jnp.zeros((MB, D), F32)
        h2t[...] = h2[...].T
        gbd_ref[...] = jnp.sum(dm[...].astype(F32), 0, keepdims=True)

    gbu_ref[...] = jnp.zeros_like(gbu_ref)

    @pl.loop(0, T // MB)
    def _(i):
        rows = rows_of(i)
        u = mm(h2[rows, :], wu_ref[...]) + bu_ref[...]
        g, slope = gelu_both(u)
        gb = g.astype(BF)
        gs[rows, :] = gb
        yacc[rows, :] += mm(gb, wd_ref[...])
        du = (mm(dm[rows, :], wd_ref[...], NT) * slope).astype(BF)
        dus[rows, :] = du
        gbu_ref[...] += jnp.sum(du.astype(F32), 0, keepdims=True)
        dacc[rows, :] += mm(du, wu_ref[...], NT)

    for t in range(FC // 256):
        cols = pl.ds(t * 256, 256)
        gwd_ref[cols, :] = mm(gs[:, cols], dm[...], TN).astype(BF)

    @pl.loop(0, D // 256)
    def _(t):
        rows = pl.ds(pl.multiple_of(t * 256, 256), 256)
        gwu_ref[rows, :] = mm(h2t[rows, :], dus[...]).astype(BF)

    @pl.when(c == FF // FC - 1)
    def _():
        gg2_ref[...] = jnp.zeros_like(gg2_ref)
        gb2_ref[...] = jnp.zeros_like(gb2_ref)
        for row in range(2):
            out_ref[row] = yacc[pl.ds(row * S, SEQ), :].astype(BF)

        @pl.loop(0, T // MB)
        def _(i):
            rows = rows_of(i)
            n2, s2 = norm_parts(x1_ref[rows, :])
            dh = dacc[rows, :]
            gg2_ref[...] += jnp.sum(dh * n2, 0, keepdims=True)
            gb2_ref[...] += jnp.sum(dh, 0, keepdims=True)
            dx1_ref[rows, :] = dm[rows, :].astype(F32) + norm_pull(dh, n2, s2, vec_ref[G2:G2 + 1, :])


def ffn(x1, dm, wide, down, bu, vec):
    one = jax.ShapeDtypeStruct((1, D), F32)
    return pl.pallas_call(
        ffn_kernel,
        grid=(FF // FC,),
        in_specs=[
            whole((T, D)), whole((2, SEQ, D)),
            pl.BlockSpec((D, FC), lambda c: (0, c + UP_AT // FC)), pl.BlockSpec((FC, D), lambda c: (c, 0)),
            pl.BlockSpec((1, FC), lambda c: (0, c)), whole((8, D)),
        ],
        out_specs=[
            whole((2, SEQ, D)), whole((T, D)),
            pl.BlockSpec((D, FC), lambda c: (0, c)), pl.BlockSpec((FC, D), lambda c: (c, 0)),
            pl.BlockSpec((1, FC), lambda c: (0, c)), whole((1, D)), whole((1, D)), whole((1, D)),
        ],
        out_shape=[
            jax.ShapeDtypeStruct((2, SEQ, D), BF), jax.ShapeDtypeStruct((T, D), F32),
            jax.ShapeDtypeStruct((D, FF), BF), jax.ShapeDtypeStruct((FF, D), BF),
            jax.ShapeDtypeStruct((1, FF), F32), one, one, one,
        ],
        scratch_shapes=[
            pltpu.VMEM((T, D), BF), pltpu.VMEM((D, T), BF), pltpu.VMEM((T, D), BF),
            pltpu.VMEM((T, D), F32), pltpu.VMEM((T, D), F32),
            pltpu.VMEM((T, FC), BF), pltpu.VMEM((T, FC), BF),
        ],
        compiler_params=pltpu.CompilerParams(vmem_limit_bytes=LIMIT),
        name="feed_forward",
    )(x1, dm, wide, down, bu, vec)


def attn_bwd_kernel(
    x_ref, dx1_ref, h1_ref, qkv_ref, p_ref, attn_ref, rl_ref, wo_ref, wqkv_ref, vec_ref,
    gx_ref, gwqkv_ref, gwo_ref, gbqkv_ref, gbo_ref, gg1_ref, gb1_ref,
    da, dos, h1t, dqkv,
):
    hq, r = pl.program_id(0), pl.program_id(1)

    @pl.when((hq == 0) & (r == 0))
    def _():
        gbo_ref[...] = jnp.zeros_like(gbo_ref)

        @pl.loop(0, T // MB)
        def _(i):
            rows = rows_of(i)
            d = dx1_ref[rows, :].astype(BF)
            da[rows, :] = d
            gbo_ref[...] += jnp.sum(d.astype(F32), 0, keepdims=True)
            dos[rows, :] = (mm(d, wo_ref[...], NT) * rl_ref[rows, :]).astype(BF)
        h1t[...] = h1_ref[...].T

    rows = pl.ds(pl.multiple_of(r * S, 16), S)
    scale = 1.0 / math.sqrt(HD)
    for j in range(HG // 2):
        at = j * 384
        qp, kp, vp = (qkv_ref[rows, at + 128 * n: at + 128 * (n + 1)] for n in range(3))
        do = dos[rows, pl.ds(pl.multiple_of(hq * QW + j * 128, 128), 128)]
        prod = do.astype(F32) * attn_ref[rows, j * 128:(j + 1) * 128].astype(F32)
        dq = dk = dv = None
        for e in range(2):
            keep = head_lanes((S, 128), e)
            zero = jnp.zeros_like(qp)
            doe = jnp.where(keep, do, zero)
            dot = jnp.sum(jnp.where(keep, prod, 0.0), -1, keepdims=True)
            p = p_ref[0, 2 * j + e]
            ds = (p.astype(F32) * (mm(doe, vp, NT) - dot)).astype(BF)
            a = mm(ds, jnp.where(keep, kp, zero))
            b = mm(ds, jnp.where(keep, qp, zero), TN)
            c = mm(p, doe, TN)
            dq, dk, dv = (a, b, c) if dq is None else (dq + a, dk + b, dv + c)
        for n, part in enumerate((dq * scale, dk * scale, dv)):
            col = hq * GW + j * 384 + n * 128
            dqkv[rows, pl.ds(pl.multiple_of(col, 128), 128)] = part.astype(BF)

    @pl.when(r == 1)
    def _():
        part = dqkv[:, pl.ds(pl.multiple_of(hq * GW, 128), GW)]
        gbqkv_ref[...] = jnp.sum(part.astype(F32), 0, keepdims=True)

        @pl.loop(0, D // 256)
        def _(t):
            rr = pl.ds(pl.multiple_of(t * 256, 256), 256)
            gwqkv_ref[rr, :] = mm(h1t[rr, :], part).astype(BF)
        gwo_ref[...] = mm(attn_ref[...], da[...], TN).astype(BF)

    @pl.when((hq == D // QW - 1) & (r == 1))
    def _():
        gg1_ref[...] = jnp.zeros_like(gg1_ref)
        gb1_ref[...] = jnp.zeros_like(gb1_ref)
        for row in range(2):
            rr = pl.ds(row * S, SEQ)
            dh = mm(dqkv[pl.ds(row * S, S), :], wqkv_ref[...], NT)[:SEQ]
            n1, s1 = norm_parts(x_ref[row].astype(F32))
            gg1_ref[...] += jnp.sum(dh * n1, 0, keepdims=True)
            gb1_ref[...] += jnp.sum(dh, 0, keepdims=True)
            gx_ref[row] = (dx1_ref[rr, :] + norm_pull(dh, n1, s1, vec_ref[G1:G1 + 1, :])).astype(BF)


def attn_bwd(x, dx1, h1, qkv, p, attn, rl, wide, vec):
    act = pl.BlockSpec((T, QW), lambda h, r: (0, h))
    one = jax.ShapeDtypeStruct((1, D), F32)
    return pl.pallas_call(
        attn_bwd_kernel,
        grid=(D // QW, 2),
        in_specs=[
            whole((2, SEQ, D)), whole((T, D)), whole((T, D)), pl.BlockSpec((T, GW), lambda h, r: (0, h)),
            pl.BlockSpec((1, HG, S, S), lambda h, r: (r, h, 0, 0)), act, whole((T, D)),
            pl.BlockSpec((D, D), lambda h, r: (0, 3)), whole((D, 3 * D)), whole((8, D)),
        ],
        out_specs=[
            whole((2, SEQ, D)), pl.BlockSpec((D, GW), lambda h, r: (0, h)),
            pl.BlockSpec((QW, D), lambda h, r: (h, 0)),
            pl.BlockSpec((1, GW), lambda h, r: (0, h)), whole((1, D)), whole((1, D)), whole((1, D)),
        ],
        out_shape=[
            jax.ShapeDtypeStruct((2, SEQ, D), BF), jax.ShapeDtypeStruct((D, 3 * D), BF), jax.ShapeDtypeStruct((D, D), BF),
            jax.ShapeDtypeStruct((1, 3 * D), F32), one, one, one,
        ],
        scratch_shapes=[
            pltpu.VMEM((T, D), BF), pltpu.VMEM((T, D), BF), pltpu.VMEM((D, T), BF), pltpu.VMEM((T, 3 * D), BF),
        ],
        compiler_params=pltpu.CompilerParams(vmem_limit_bytes=LIMIT),
        name="attention_backward",
    )(x, dx1, h1, qkv, p, attn, rl, wide, wide, vec)


NZ = 4
CH = 48
HW = 384
SW = 384
N_WIDE = AW // (2 * HW)
N_DOWN = 2
N_UP = FF // D
DH = 2 * CH
NV = 8
VW = (24,) * NV + (96,)


def one(i):
    return pl.ds(i, 1)


EVERY = pl.ds(0, NZ)
TWO = pl.ds(0, 2)


def where_am_i():
    dp, fs = lax.axis_index("dp"), lax.axis_index("fsdp")
    return lax.div(dp, 2), lax.rem(dp, 2), lax.div(fs, 2), lax.rem(fs, 2)


def device(z, x, y, c):
    return (z * 2 + x, y * 2 + c)


def partners(z, x, y, c):
    found = [device(lax.rem(z + k, NZ), x, y, c) for k in (1, 2, 3)]
    return found + [device(z, 1 - x, y, c), device(z, x, 1 - y, c), device(z, x, y, 1 - c)]


def say_hello(here):
    barrier = pltpu.get_barrier_semaphore()
    for other in partners(*here):
        pl.semaphore_signal(barrier, inc=1, device_id=other, device_id_type=MESH)


def await_all():
    pl.semaphore_wait(pltpu.get_barrier_semaphore(), 6)


def remote(src, dst, sems, n, target):
    return pltpu.make_async_remote_copy(
        src_ref=src, dst_ref=dst, send_sem=sems[0].at[n], recv_sem=sems[1].at[n],
        device_id=target, device_id_type=MESH,
    )


def half(i, core):
    return pl.ds(pl.multiple_of(i * 2 * HW + core * HW, 128), HW)


def add(a, b):
    return (a.astype(F32) + b.astype(F32)).astype(BF)


def plan(entries, ticks):
    table = {n: [] for n in range(len(ticks))}
    for due, action in sorted(entries, key=lambda e: e[0]):
        table[min((n for n, t in enumerate(ticks) if t >= due), default=len(ticks) - 1)].append(action)
    return table


class Gather:
    COPIES = 7

    def __init__(self, here, sems, base, view, first):
        z, x, y, c = here
        peers = partners(*here)
        mine = view(one(z), one(x), one(y))
        column = view(EVERY, one(x), one(y))
        fx, fy = jnp.where(c == 0, 1 - x, x), jnp.where(c == 0, y, 1 - y)
        tx, ty = jnp.where(c == 0, x, 1 - x), jnp.where(c == 0, 1 - y, y)
        passed = view(EVERY, one(fx), one(fy))
        all_of = view(EVERY, TWO, TWO)
        make = lambda n, src, dst, to: remote(src, dst, sems, base + n, to)
        self.along_z = [make(k, mine if first is None else first, mine, peers[k]) for k in range(3)]
        self.along_x = make(3, column, column, peers[3])
        self.along_y = make(4, column, column, peers[4])
        self.diagonal = make(5, passed, passed, device(z, tx, ty, c))
        self.sibling = make(6, all_of, all_of, peers[5])

    def start(self, phase):
        if phase == 0:
            for copy in self.along_z:
                copy.start()
        elif phase == 1:
            for copy in self.along_z:
                copy.wait_recv()
            self.along_x.start()
            self.along_y.start()
        elif phase == 2:
            self.along_x.wait_recv()
            self.along_y.wait_recv()
            self.diagonal.start()
        elif phase == 3:
            self.diagonal.wait_recv()
            self.sibling.start()
        else:
            self.sibling.wait_recv()

    def drain(self):
        for copy in (*self.along_z, self.along_x, self.along_y, self.diagonal, self.sibling):
            copy.wait_send()


class Scatter:
    COPIES = 7

    def __init__(self, here, sems, base, theirs, mine, acc, via, last, zs):
        self.mine, self.acc, self.via, self.last, self.zs = mine, acc, via, last, zs
        z, x, y, c = self.here = here
        peers = partners(*here)
        ix, iy = jnp.where(c == 0, x, 1 - x), jnp.where(c == 0, 1 - y, y)
        self.px, self.py = jnp.where(c == 0, 1 - x, x), jnp.where(c == 0, y, 1 - y)
        first, second = device(z, ix, iy, c), device(z, self.px, self.py, c)
        make = lambda n, src, dst, to: remote(src, dst, sems, base + n, to)
        at = lambda xs, ys: acc.at[EVERY, one(xs), one(ys)]
        self.swap = make(0, theirs, acc, peers[5])
        self.far = make(1, at(1 - x, 1 - y), via.at[0], first)
        self.near = make(2, at(ix, iy), via.at[1], first)
        self.next = make(3, at(self.px, self.py), last, second)
        self.along_z = [
            make(4 + k, acc.at[one(lax.rem(z + k + 1, NZ)), one(x), one(y)], zs.at[k], peers[k]) for k in range(3)
        ]

    def start(self, phase):
        z, x, y, c = self.here
        acc = self.acc
        if phase == 0:
            self.swap.start()
        elif phase == 1:
            self.swap.wait_recv()

            @pl.loop(0, NZ)
            def _(i):
                for xi in range(2):
                    for yi in range(2):
                        acc[i, xi, yi] = add(acc[i, xi, yi], self.mine(i, xi, yi))
            self.far.start()
            self.near.start()
        elif phase == 2:
            self.far.wait_recv()
            px, py = self.px, self.py

            @pl.loop(0, NZ)
            def _(i):
                acc[i, px, py] = add(acc[i, px, py], self.via[0, i, 0, 0])
            self.next.start()
            self.near.wait_recv()

            @pl.loop(0, NZ)
            def _(i):
                acc[i, x, y] = add(acc[i, x, y], self.via[1, i, 0, 0])
        elif phase == 3:
            self.next.wait_recv()

            @pl.loop(0, NZ)
            def _(i):
                acc[i, x, y] = add(acc[i, x, y], self.last[i, 0, 0])
            for copy in self.along_z:
                copy.start()

    def total(self):
        z, x, y, c = self.here
        for copy in self.along_z:
            copy.wait_recv()
        parts = [self.acc[z, x, y]] + [self.zs[k, 0, 0, 0] for k in range(3)]
        return sum(part.astype(F32) for part in parts)

    def drain(self):
        for copy in (self.swap, self.far, self.near, self.next, *self.along_z):
            copy.wait_send()


def scatter_bufs(n, width):
    return [
        pltpu.VMEM((n, NZ, 2, 2, CH, width), BF), pltpu.VMEM((n, 2, NZ, 1, 1, CH, width), BF),
        pltpu.VMEM((n, NZ, 1, 1, CH, width), BF), pltpu.VMEM((n, 3, 1, 1, 1, CH, width), BF),
    ]


def dma_sems(*counts):
    return [pltpu.SemaphoreType.DMA((k,)) for k in counts]


def fixed(shape):
    return pl.BlockSpec(shape, lambda s: (0,) * len(shape), pipeline_mode=pl.Buffered(1))


def vmem():
    return pl.BlockSpec(memory_space=pltpu.VMEM)


def hbm():
    return pl.BlockSpec(memory_space=pl.ANY)


N_ATT = 2 * (D // QW)
FORWARD_TICKS = [2.9 * n for n in range(20)]


def forward_kernel(
    kind_ref, x_ref, dm_ref, wqkv_ref, wout_ref, wup_ref, wdown_ref, *refs,
):
    small_refs = refs[:NV + 1]
    (
        h1t_ref, qkv_ref, p_ref, attn_ref, rl_ref, x1_ref, dmp_ref, h2t_ref, g_ref, slope_ref, gdown_ref,
        vec_ref, watt_out, wup_out, down_out,
        fa, fb, h1, h2, staged, swap, watt, wup, bqkv, bu, smalls,
        sems_s, sems_r, swap_s, swap_r, small_s, small_r, copy_sem,
    ) = refs[NV + 1:]
    step = pl.program_id(0)
    here = where_am_i()
    z, x, y, c = here
    peers = partners(*here)
    sems = (sems_s, sems_r)

    swaps = [
        remote(staged.at[:, half(i, 1 - c)], swap.at[:, i * HW:(i + 1) * HW], (swap_s, swap_r), i, peers[5])
        for i in range(N_WIDE)
    ]
    items, own = [], []
    for i in range(N_WIDE):
        buf, at = (watt, i) if i < 4 else (wup, i - 4)
        view = lambda zs, xs, ys, buf=buf, at=at: buf.at[zs, xs, ys, :, half(at, c)]
        items.append(Gather(here, sems, i * Gather.COPIES, view, None))
    for i in range(N_DOWN):
        rows = pl.ds(pl.multiple_of(c * DH + i * CH, 16), CH)
        view = lambda zs, xs, ys, rows=rows: down_out.at[zs, xs, ys, rows]
        first = wdown_ref.at[:, :, :, pl.ds(i * CH, CH)]
        items.append(Gather(here, sems, (N_WIDE + i) * Gather.COPIES, view, first))
        own.append(pltpu.make_async_copy(first, view(one(z), one(x), one(y)), copy_sem.at[N_WIDE + i]))
    keeps = []
    for i in range(N_WIDE):
        src, dst, at = (watt, watt_out, i) if i < 4 else (wup, wup_out, i - 4)
        cols = pl.ds(at * D, D)
        keeps.append(pltpu.make_async_copy(
            src.at[:, :, :, :, cols], dst.at[:, :, :, :, cols], copy_sem.at[i]))

    def act(action):
        i, phase = action
        if i >= N_WIDE and phase == 1:
            own[i - N_WIDE].wait()
        items[i].start(phase)
        if phase == 4 and i < N_WIDE:
            keeps[i].start()

    LAG = (0.0, 0.0, 6.0, 10.0, 14.0)
    entries = []
    begin = -10.0
    for i in range(1, N_WIDE + N_DOWN):
        length = 4.9 if i < N_WIDE else 9.8
        for phase in range(1, 5):
            due = begin + LAG[phase] * (length / 4.9 if i >= N_WIDE else 1.0)
            if phase == 4 and i < N_WIDE:
                due = min(due, FORWARD_TICKS[(4, 8, 11, 12, 14, 16, 18)[i - 1]])
            entries.append((due, (i, phase)))
        begin += length
    early = [a for t, a in sorted(entries, key=lambda e: e[0]) if t < 0.0]
    table = plan([e for e in entries if e[0] >= 0.0], FORWARD_TICKS)

    def tick(part):
        for s in range(10):
            todo = table[2 * s + part]
            if todo:
                @pl.when(step == s)
                def _(todo=todo):
                    for action in todo:
                        act(action)

    @pl.when(step == 0)
    def _():
        say_hello(here)
        for pair in range(6):
            for n in range(3):
                at = pair * 384 + n * 128
                staged[:, at:at + 128] = wqkv_ref[:, n * D + pair * 128:n * D + (pair + 1) * 128].astype(F32)
        staged[:, OUT_AT:UP_AT] = wout_ref[...].astype(F32)
        staged[:, UP_AT:] = wup_ref[...].astype(F32)
        at = 0
        line = smalls.at[z, x, y, c]
        line[...] = jnp.zeros((8, SW), F32)
        for ref, width in zip(small_refs, VW):
            line[0:1, at:at + width] = ref[...].astype(F32).reshape(1, width)
            at += width
        await_all()
        swaps[0].start()

        def small_copy(n, src, to):
            return remote(src, src, (small_s, small_r), n, to)

        small_c = small_copy(0, smalls.at[one(z), one(x), one(y), one(c)], peers[5])
        both = smalls.at[one(z), one(x), one(y), TWO]
        small_z = [small_copy(1 + k, both, peers[k]) for k in range(3)]
        small_x = small_copy(4, smalls.at[EVERY, one(x), one(y), TWO], peers[3])
        small_y = small_copy(5, smalls.at[EVERY, TWO, one(y), TWO], peers[4])
        small_c.start()
        for i in range(1, N_WIDE):
            swaps[i].start()
        for i in range(N_WIDE):
            swaps[i].wait_recv()
            mine_part = staged[:, half(i, c)]
            their_part = swap[:, i * HW:(i + 1) * HW]
            buf, at = (watt, i) if i < 4 else (wup, i - 4)
            lower = jnp.where(c == 0, mine_part, their_part)
            upper = jnp.where(c == 0, their_part, mine_part)
            buf[z, x, y, :, half(at, c)] = jnp.concatenate([lower, upper], 0).astype(BF)
            items[i].start(0)
            if i == 0:
                small_c.wait_recv()
                for copy in small_z:
                    copy.start()
        for i in range(N_DOWN):
            items[N_WIDE + i].start(0)
            own[i].start()

        def take_row(row):
            for ref in (x1_ref, dmp_ref):
                ref[pl.ds(row * S + S - 16, 16), :] = jnp.zeros((16, D), ref.dtype)
            x1_ref[pl.ds(row * S, SEQ), :] = x_ref[:, row, :].astype(F32)

        items[0].start(1)
        for copy in small_z:
            copy.wait_recv()
        small_x.start()
        take_row(0)
        items[0].start(2)
        small_x.wait_recv()
        small_y.start()
        take_row(1)
        for row in range(2):
            dmp_ref[pl.ds(row * S, SEQ), :] = dm_ref[:, row, :]
        items[0].start(3)
        for action in early:
            act(action)
        small_y.wait_recv()
        pieces = smalls[...].reshape(32, 8, SW)[:, 0, :].astype(BF)

        def joined(lead, size, width):
            src = lax.broadcasted_iota(jnp.int32, (SW, size), 0)
            dst = lax.broadcasted_iota(jnp.int32, (SW, size), 1)
            spread = jnp.where(src == lead + lax.rem(dst, width), 1.0, 0.0).astype(BF)
            dev = lax.broadcasted_iota(jnp.int32, (32, size), 0)
            col = lax.broadcasted_iota(jnp.int32, (32, size), 1)
            return jnp.sum(jnp.where(lax.div(col, width) == dev, mm(pieces, spread), 0.0), 0, keepdims=True)

        vectors = [joined(24 * i, D, 24) for i in range(NV)]
        for i in range(NV):
            vec_ref[i:i + 1, :] = vectors[i]
        for part in range(N_UP):
            src = lax.broadcasted_iota(jnp.int32, (SW, D), 0)
            dst = lax.broadcasted_iota(jnp.int32, (SW, D), 1)
            spread = jnp.where(src == 24 * NV + lax.rem(dst, 96), 1.0, 0.0).astype(BF)
            dev = lax.broadcasted_iota(jnp.int32, (32, D), 0)
            col = lax.broadcasted_iota(jnp.int32, (32, D), 1)
            found = jnp.where(lax.div(col, 96) + 8 * part == dev, mm(pieces, spread), 0.0)
            bu[part] = jnp.sum(found, 0, keepdims=True)
        for pair in range(6):
            n, at = pair // 2, (pair % 2) * 384
            bqkv[n, :, at:at + 128] = vectors[BQ][:, pair * 128:(pair + 1) * 128]
            bqkv[n, :, at + 128:at + 256] = jnp.zeros((1, 128), F32)
            bqkv[n, :, at + 256:at + 384] = vectors[BV][:, pair * 128:(pair + 1) * 128]

        @pl.loop(0, T // MB)
        def _(i):
            rows = rows_of(i)
            n1, _s = norm_parts(x1_ref[rows, :])
            h1[rows, :] = (n1 * vec_ref[G1:G1 + 1, :] + vec_ref[B1:B1 + 1, :]).astype(BF)
        for row in range(2):
            slot = lax.broadcasted_iota(jnp.int32, (S, 128), 0)
            lane = lax.broadcasted_iota(jnp.int32, (S, 128), 1)
            packed = jnp.where(slot < HALF, 0, jnp.where(slot < 2 * HALF, 1, 2))
            seg = jnp.where(kind_ref[row] == 1, packed, 0)
            fa[row] = jnp.where((lane < 3) & (seg == lane), -1e30, 0.0).astype(BF)
            fb[row] = jnp.where((lane < 3) & ((seg != lane) | (slot >= SEQ)), 1.0, 0.0).astype(BF)
        h1t_ref[...] = h1[...].T
        rl_ref[...] = jnp.zeros_like(rl_ref)
        act((0, 4))
        for copy in (small_c, *small_z, small_x, small_y, *swaps):
            copy.wait_send()

    tick(0)

    @pl.when(step < N_ATT)
    def _():
        hq, r = lax.div(step, 2), lax.rem(step, 2)

        @pl.when(r == 0)
        def _():
            @pl.loop(0, T // MB)
            def _(i):
                rows = rows_of(i)
                w = watt[:, :, :, :, pl.ds(pl.multiple_of(hq * GW, 128), GW)].reshape(D, GW)
                qkv_ref[rows, :] = (mm(h1[rows, :], w) + bqkv[hq]).astype(BF)

        rows = pl.ds(pl.multiple_of(r * S, 16), S)
        feat_q, feat_k = fa[r], fb[r]
        ones = jnp.ones((S, 128), BF)
        scale = math.log2(math.e) / math.sqrt(HD)
        for j in range(HG // 2):
            if j:
                tick(1)
            at = j * 384
            qp, kp, vp = (qkv_ref[rows, at + 128 * n: at + 128 * (n + 1)] for n in range(3))
            kcat = jnp.concatenate([kp, feat_k], 1)
            total = None
            for e in range(2):
                keep = head_lanes((S, 128), e)
                qcat = jnp.concatenate([jnp.where(keep, qp, jnp.zeros_like(qp)), feat_q], 1)
                s = mm(qcat, kcat, NT)
                m = jnp.max(s, -1, keepdims=True)
                pb = jnp.exp2((s - m) * scale).astype(BF)
                p_ref[0, 2 * j + e] = pb
                vcat = jnp.concatenate([jnp.where(keep, vp, jnp.zeros_like(vp)), ones], 1)
                o = mm(pb, vcat)
                rl = 1.0 / o[:, 128:]
                part = o[:, :128] * rl
                total = part if total is None else total + part
                spot = lax.broadcasted_iota(jnp.int32, (S, 128), 1) == hq * HG + 2 * j + e
                rl_ref[rows, :] = jnp.where(spot, rl, rl_ref[rows, :])
            out = pl.ds(pl.multiple_of(hq * QW + j * 128, 128), 128)
            attn_ref[rows, out] = total.astype(BF)

    @pl.when(step == N_ATT - 1)
    def _():
        @pl.loop(0, T // MB)
        def _(i):
            rows = rows_of(i)
            wo = watt[:, :, :, :, OUT_AT:UP_AT].reshape(D, D)
            x1 = x1_ref[rows, :] + mm(attn_ref[rows, :], wo) + vec_ref[BO:BO + 1, :]
            x1_ref[rows, :] = x1
            n2, _s = norm_parts(x1)
            h2[rows, :] = (n2 * vec_ref[G2:G2 + 1, :] + vec_ref[B2:B2 + 1, :]).astype(BF)
        h2t_ref[...] = h2[...].T

    @pl.when(step >= N_ATT)
    def _():
        part = step - N_ATT

        def hidden(i):
            rows = rows_of(i)
            w = wup[:, :, :, :, pl.ds(pl.multiple_of(part * D, 128), D)].reshape(D, D)
            g, slope = gelu_both(mm(h2[rows, :], w) + bu[part])
            g_ref[rows, :] = g.astype(BF)
            slope_ref[rows, :] = slope.astype(BF)

        pl.loop(0, T // MB // 2)(hidden)
        tick(1)
        pl.loop(T // MB // 2, T // MB)(hidden)
        for t in range(D // 256):
            cols = pl.ds(t * 256, 256)
            gdown_ref[cols, :] = mm(g_ref[:, cols], dmp_ref[...], TN).astype(BF)

    @pl.when(step == 9)
    def _():
        for item in items:
            item.drain()
        for copy in keeps:
            copy.wait()


def forward(kind, x, dm, wqkv, wout, wup, wdown, smalls):
    n = N_WIDE + N_DOWN
    att = lambda s: jnp.minimum(s, N_ATT - 1)
    ff = lambda s: jnp.maximum(s - N_ATT, 0)
    shape = jax.ShapeDtypeStruct
    return pl.pallas_call(
        forward_kernel,
        grid=(N_ATT + N_UP,),
        in_specs=[
            pl.BlockSpec(memory_space=pltpu.SMEM), fixed((SEQ, 2, D)), fixed((SEQ, 2, D)),
            fixed((24, 3 * D)), fixed((24, D)), fixed((24, FF)), fixed((1, 1, 1, 96, D)),
            *[pl.BlockSpec((w,), lambda s: (0,), pipeline_mode=pl.Buffered(1)) for w in VW],
        ],
        out_specs=[
            fixed((D, T)), pl.BlockSpec((T, GW), lambda s: (0, att(s) // 2)),
            pl.BlockSpec((1, HG, S, S), lambda s: (att(s) % 2, att(s) // 2, 0, 0)),
            fixed((T, D)), fixed((T, 128)), fixed((T, D)), fixed((T, D)), fixed((D, T)),
            pl.BlockSpec((T, D), lambda s: (0, ff(s))), pl.BlockSpec((T, D), lambda s: (0, ff(s))),
            pl.BlockSpec((D, D), lambda s: (ff(s), 0)),
            fixed((NV, D)), hbm(), hbm(), hbm(),
        ],
        out_shape=[
            shape((D, T), BF), shape((T, 3 * D), BF), shape((2, D // HD, S, S), BF),
            shape((T, D), BF), shape((T, 128), F32), shape((T, D), F32), shape((T, D), BF), shape((D, T), BF),
            shape((T, FF), BF), shape((T, FF), BF), shape((FF, D), BF), shape((NV, D), F32),
            shape((NZ, 2, 2, CH, UP_AT), BF), shape((NZ, 2, 2, CH, FF), BF), shape((NZ, 2, 2, 4 * CH, D), BF),
        ],
        scratch_shapes=[
            pltpu.VMEM((2, S, 128), BF), pltpu.VMEM((2, S, 128), BF), pltpu.VMEM((T, D), BF), pltpu.VMEM((T, D), BF),
            pltpu.VMEM((24, AW), F32), pltpu.VMEM((24, AW // 2), F32),
            pltpu.VMEM((NZ, 2, 2, CH, UP_AT), BF), pltpu.VMEM((NZ, 2, 2, CH, FF), BF),
            pltpu.VMEM((3, 1, GW), F32), pltpu.VMEM((N_UP, 1, D), F32), pltpu.VMEM((NZ, 2, 2, 2, 8, SW), F32),
            *dma_sems(n * Gather.COPIES, n * Gather.COPIES, N_WIDE, N_WIDE, 6, 6, n),
        ],
        compiler_params=pltpu.CompilerParams(collective_id=0, has_side_effects=True, vmem_limit_bytes=LIMIT),
        name="forward",
    )(kind, x, dm, wqkv, wout, wup, wdown.reshape(1, 1, 1, 96, D), *smalls)


def ffn_back_kernel(
    x1_ref, dm_ref, g_ref, slope_ref, wu_ref, wd_ref, h2t_ref, vec_ref, gdown_ref,
    y_ref, dx1_ref, gup_ref, sums_ref, odown_ref,
    yacc, dacc, dus, mine, acc, via, last, zs, sems_s, sems_r, own_sem,
):
    step = pl.program_id(0)
    here = where_am_i()
    z, x, y, c = here
    items, own = [], []
    for i in range(N_DOWN):
        rows = lambda core, i=i: pl.ds(pl.multiple_of(core * DH + i * CH, 16), CH)
        own.append(pltpu.make_async_copy(gdown_ref.at[:, :, :, rows(c)], mine.at[i], own_sem.at[i]))
        items.append(Scatter(
            here, (sems_s, sems_r), i * Scatter.COPIES, gdown_ref.at[EVERY, TWO, TWO, rows(1 - c)],
            lambda a, b, d, i=i: mine[i, a, b, d], acc.at[i], via.at[i], last.at[i], zs.at[i],
        ))

    @pl.when(step == 0)
    def _():
        say_hello(here)
        for copy in own:
            copy.start()

        @pl.loop(0, T // MB)
        def _(i):
            rows = rows_of(i)
            yacc[rows, :] = x1_ref[rows, :] + vec_ref[BD:BD + 1, :]
            dacc[rows, :] = jnp.zeros((MB, D), F32)
        sums_ref[...] = jnp.zeros_like(sums_ref)
        sums_ref[2:3, :] = jnp.sum(dm_ref[...].astype(F32), 0, keepdims=True)
        await_all()
        for item in items:
            item.start(0)

    for s in range(1, N_UP):
        @pl.when(step == s)
        def _(s=s):
            for i, item in enumerate(items):
                if s == 1:
                    own[i].wait()
                item.start(s)

    def block(i):
        rows = rows_of(i)
        g = g_ref[rows, :]
        yacc[rows, :] += mm(g, wd_ref[...])
        du = (mm(dm_ref[rows, :], wd_ref[...], NT) * slope_ref[rows, :].astype(F32)).astype(BF)
        dus[rows, :] = du
        sums_ref[pl.ds(3 + step, 1), :] += jnp.sum(du.astype(F32), 0, keepdims=True)
        dacc[rows, :] += mm(du, wu_ref[...], NT)

    pl.loop(0, T // MB)(block)

    @pl.loop(0, D // 256)
    def _(t):
        rows = pl.ds(pl.multiple_of(t * 256, 256), 256)
        gup_ref[rows, :] = mm(h2t_ref[rows, :], dus[...]).astype(BF)

    @pl.when(step == N_UP - 1)
    def _():
        @pl.loop(0, T // MB)
        def _(i):
            rows = rows_of(i)
            n2, s2 = norm_parts(x1_ref[rows, :])
            dh = dacc[rows, :]
            sums_ref[0:1, :] += jnp.sum(dh * n2, 0, keepdims=True)
            sums_ref[1:2, :] += jnp.sum(dh, 0, keepdims=True)
            dx1_ref[rows, :] = dm_ref[rows, :].astype(F32) + norm_pull(dh, n2, s2, vec_ref[G2:G2 + 1, :])
            y_ref[rows, :] = yacc[rows, :].astype(BF)
        for i, item in enumerate(items):
            odown_ref[pl.ds(i * CH, CH), :] = item.total()
            item.drain()


def ffn_back(x1, dm, g, slope, wup, down, h2t, vec, gdown):
    shape = jax.ShapeDtypeStruct
    col = pl.BlockSpec((T, D), lambda s: (0, s))
    return pl.pallas_call(
        ffn_back_kernel,
        grid=(N_UP,),
        in_specs=[
            fixed((T, D)), fixed((T, D)), col, col,
            pl.BlockSpec((D, D), lambda s: (0, s)), pl.BlockSpec((D, D), lambda s: (s, 0)),
            fixed((D, T)), fixed((NV, D)), hbm(),
        ],
        out_specs=[
            fixed((T, D)), fixed((T, D)), pl.BlockSpec((D, D), lambda s: (0, s)), fixed((8, D)), fixed((96, D)),
        ],
        out_shape=[
            shape((T, D), BF), shape((T, D), F32), shape((D, FF), BF), shape((8, D), F32), shape((96, D), F32),
        ],
        scratch_shapes=[
            pltpu.VMEM((T, D), F32), pltpu.VMEM((T, D), F32), pltpu.VMEM((T, D), BF),
            pltpu.VMEM((N_DOWN, NZ, 2, 2, CH, D), BF), *scatter_bufs(N_DOWN, D),
            *dma_sems(N_DOWN * 7, N_DOWN * 7, N_DOWN),
        ],
        compiler_params=pltpu.CompilerParams(collective_id=1, has_side_effects=True, vmem_limit_bytes=LIMIT),
        name="feed_forward_back",
    )(x1, dm, g, slope, wup, down, h2t, vec, gdown.reshape(NZ, 2, 2, 4 * CH, D))


BACK_TICKS = [4.0 * n for n in range(12)]
N_BACK = N_UP + 4


def attn_back_kernel(
    x_ref, yb_ref, dx1_ref, h1t_ref, qkv_ref, p_ref, attn_ref, rl_ref, wo_ref, wqkv_ref, vec_ref, sums_ref, gup_ref,
    out_ref, gx_ref, oqkv_ref, oout_ref, oup_ref, *refs,
):
    small_outs = refs[:NV + 1]
    (
        da, dos, dqkv, dh1, gqkv, gout, mine, acc, via, last, zs, done, landed, small,
        sems_s, sems_r, fin_s, fin_r, small_s, small_r, own_sem,
    ) = refs[NV + 1:]
    step = pl.program_id(0)
    hq, r = lax.div(step, 2), lax.rem(step, 2)
    here = where_am_i()
    z, x, y, c = here
    peers = partners(*here)
    items, own = [], []
    for n in range(N_BACK):
        if n < N_UP:
            theirs = gup_ref.at[EVERY, TWO, TWO, :, half(n, 1 - c)]
            own.append(pltpu.make_async_copy(gup_ref.at[:, :, :, :, half(n, c)], mine.at[n], own_sem.at[n]))
            get = lambda a, b, d, n=n: mine[n, a, b, d]
        elif n == N_UP:
            theirs = gout.at[EVERY, TWO, TWO, :, half(0, 1 - c)]
            get = lambda a, b, d: gout[a, b, d, :, half(0, c)]
        else:
            i = n - N_UP - 1
            theirs = gqkv.at[i, EVERY, TWO, TWO, :, half(0, 1 - c)]
            get = lambda a, b, d, i=i: gqkv[i, a, b, d, :, half(0, c)]
        items.append(Scatter(
            here, (sems_s, sems_r), n * Scatter.COPIES, theirs, get, acc.at[n], via.at[n], last.at[n], zs.at[n]))

    def final(n):
        theirs = pl.ds(pl.multiple_of((1 - c) * 24, 8), 24)
        return remote(done.at[n, theirs], landed.at[n], (fin_s, fin_r), n, peers[5])

    def put(n, core, value):
        if n > N_UP:
            for b in range(3):
                cols = pl.ds(pl.multiple_of(b * D + (n - N_UP - 1) * QW + core * 128, 128), 128)
                oqkv_ref[:, cols] = value[:, b * 128:(b + 1) * 128]
        elif n == N_UP:
            oout_ref[:, half(0, core)] = value
        else:
            oup_ref[:, half(n, core)] = value

    def finish(n):
        done[n] = items[n].total()
        final(n).start()
        put(n, c, done[n, pl.ds(pl.multiple_of(c * 24, 8), 24)])

    def act(action):
        n, phase = action
        if n < N_UP and phase == 1:
            own[n].wait()
        if phase == 4:
            finish(n)
        else:
            items[n].start(phase)

    LAG = (0.0, 3.0, 8.0, 11.0, 17.0)
    entries = []
    begin = 0.0
    for n in range(N_BACK):
        if n == N_UP + 1:
            begin = max(begin, BACK_TICKS[4])
        if n == N_UP + 2:
            begin = max(begin, BACK_TICKS[8])
        if n == N_UP + 3:
            begin = max(begin, BACK_TICKS[-1] + 4.0)
        for phase in range(1, 5):
            entries.append((begin + LAG[phase], (n, phase)))
        begin += 4.9
    tail = [a for t, a in sorted(entries, key=lambda e: e[0]) if t > BACK_TICKS[-1] or a[0] == N_BACK - 1]
    table = plan([e for e in entries if e[0] <= BACK_TICKS[-1] and e[1][0] != N_BACK - 1], BACK_TICKS)

    def tick(part):
        for s in range(N_ATT):
            todo = table[2 * s + part]
            if todo:
                @pl.when(step == s)
                def _(todo=todo):
                    for action in todo:
                        act(action)

    @pl.when(step == 0)
    def _():
        say_hello(here)
        for copy in own:
            copy.start()
        small[0] = jnp.zeros((16, D), F32)
        await_all()
        for n in range(N_UP):
            items[n].start(0)

        src = lax.broadcasted_iota(jnp.int32, (128, D), 0)
        dst = lax.broadcasted_iota(jnp.int32, (128, D), 1)
        spread = jnp.where(lax.div(dst, HD) == src, 1.0, 0.0)

        @pl.loop(0, T // MB)
        def _(i):
            rows = rows_of(i)
            d = dx1_ref[rows, :].astype(BF)
            da[rows, :] = d
            rl = lax.dot_general(
                rl_ref[rows, :], spread, NN, precision=lax.Precision.HIGHEST, preferred_element_type=F32)
            small[0, 4:5, :] += jnp.sum(d.astype(F32), 0, keepdims=True)
            dos[rows, :] = (mm(d, wo_ref[...], NT) * rl).astype(BF)
            dh1[rows, :] = jnp.zeros((MB, D), F32)
        for t in range(D // 192):
            cols = pl.ds(t * 192, 192)
            part = mm(attn_ref[:, t * 192:(t + 1) * 192], da[...], TN)
            gout[t] = part.astype(BF).reshape(2, 2, CH, D)
        items[N_UP].start(0)

    tick(0)
    rows = pl.ds(pl.multiple_of(r * S, 16), S)
    scale = 1.0 / math.sqrt(HD)
    for j in range(HG // 2):
        if j:
            tick(1)
        at = j * 384
        qp, kp, vp = (qkv_ref[rows, at + 128 * n: at + 128 * (n + 1)] for n in range(3))
        lanes = pl.ds(pl.multiple_of(hq * QW + j * 128, 128), 128)
        do = dos[rows, lanes]
        prod = do.astype(F32) * attn_ref[rows, lanes].astype(F32)
        dq = dk = dv = None
        for e in range(2):
            keep = head_lanes((S, 128), e)
            zero = jnp.zeros_like(qp)
            doe = jnp.where(keep, do, zero)
            dot = jnp.sum(jnp.where(keep, prod, 0.0), -1, keepdims=True)
            p = p_ref[0, 2 * j + e]
            ds = (p.astype(F32) * (mm(doe, vp, NT) - dot)).astype(BF)
            a_, b_, c_ = mm(ds, jnp.where(keep, kp, zero)), mm(ds, jnp.where(keep, qp, zero), TN), mm(p, doe, TN)
            dq, dk, dv = (a_, b_, c_) if dq is None else (dq + a_, dk + b_, dv + c_)
        for n, part in enumerate((dq * scale, dk * scale, dv)):
            dqkv[rows, at + 128 * n:at + 128 * (n + 1)] = part.astype(BF)

    @pl.when(r == 1)
    def _():
        sums = jnp.sum(dqkv[...].astype(F32), 0, keepdims=True)
        for j in range(2):
            cols = pl.ds(pl.multiple_of(hq * QW + j * 128, 128), 128)
            small[0, 2:3, cols] = sums[:, j * 384:j * 384 + 128]
            small[0, 3:4, cols] = sums[:, j * 384 + 256:j * 384 + 384]
        for t in range(D // 192):
            part = mm(h1t_ref[t * 192:(t + 1) * 192, :], dqkv[...])
            gqkv[hq, t] = part.astype(BF).reshape(2, 2, CH, GW)
        for i in range(3):
            @pl.when(hq == i)
            def _(i=i):
                items[N_UP + 1 + i].start(0)

        @pl.loop(0, T // MB)
        def _(i):
            rr = rows_of(i)
            dh1[rr, :] += mm(dqkv[rr, :], wqkv_ref[...], NT)

    @pl.when(step == N_ATT - 1)
    def _():
        rest = list(tail)
        act(rest.pop(0))

        def norm_row(row):
            rr = pl.ds(row * S, SEQ)
            dh = dh1[rr, :]
            n1, s1 = norm_parts(x_ref[:, row, :].astype(F32))
            small[0, 0:1, :] += jnp.sum(dh * n1, 0, keepdims=True)
            small[0, 1:2, :] += jnp.sum(dh, 0, keepdims=True)
            gx_ref[:, row, :] = (dx1_ref[rr, :] + norm_pull(dh, n1, s1, vec_ref[G1:G1 + 1, :])).astype(BF)

        norm_row(0)
        norm_row(1)
        small[0, 5:12, :] = sums_ref[0:7, :]
        copies = []

        def send_small(n, src, dst, to):
            copy = remote(small.at[src], small.at[dst], (small_s, small_r), n, to)
            copy.start()
            copies.append(copy)

        send_small(0, 0, 1, peers[5])
        hops = [(1, 2, 3, peers[3]), (2, 4, 5, peers[4])]
        level = 0
        while rest or level < 4:
            if rest:
                act(rest.pop(0))
            if level == 0:
                for row in range(2):
                    out_ref[:, row, :] = yb_ref[pl.ds(row * S, SEQ), :]
            if level < 2:
                copies[level].wait_recv()
                small[2 * level + 2] = small[2 * level] + small[2 * level + 1]
                send_small(*hops[level])
            elif level == 2:
                copies[2].wait_recv()
                small[6] = small[4] + small[5]
                for k in range(3):
                    send_small(3 + k, 6, 7 + k, peers[k])
            elif level == 3:
                for k in range(3):
                    copies[3 + k].wait_recv()
                total = small[6] + small[7] + small[8] + small[9]
                me = lax.axis_index("dp") * lax.axis_size("fsdp") + lax.axis_index("fsdp")
                src = lax.broadcasted_iota(jnp.int32, (D, 128), 0)
                dst = lax.broadcasted_iota(jnp.int32, (D, 128), 1)

                def pick(lines, width, at):
                    chosen = jnp.where((src == at + dst) & (dst < width), 1.0, 0.0)
                    return lax.dot_general(
                        lines, chosen, NN, precision=lax.Precision.HIGHEST, preferred_element_type=F32)

                mine_of = pick(total[:8], 24, me * 24)
                for n in range(NV):
                    small_outs[n][...] = mine_of[n, :24]
                row = lax.broadcasted_iota(jnp.int32, (8, D), 0)
                longest = jnp.sum(jnp.where(row == lax.div(me, 8), total[8:16], 0.0), 0, keepdims=True)
                small_outs[NV][...] = pick(jnp.broadcast_to(longest, (8, D)), 96, lax.rem(me, 8) * 96)[0, :96]
            level += 1
        for n in range(N_BACK):
            copy = final(n)
            copy.wait_recv()
            put(n, 1 - c, landed[n])
            copy.wait_send()
            items[n].drain()
        for copy in copies:
            copy.wait_send()


def attn_back(x, yb, dx1, h1t, qkv, p, attn, rl, watt, vec, sums, gup):
    shape = jax.ShapeDtypeStruct
    n_fin = N_BACK
    return pl.pallas_call(
        attn_back_kernel,
        grid=(N_ATT,),
        in_specs=[
            fixed((SEQ, 2, D)), fixed((T, D)), fixed((T, D)), fixed((D, T)), pl.BlockSpec((T, GW), lambda s: (0, s // 2)),
            pl.BlockSpec((1, HG, S, S), lambda s: (s % 2, s // 2, 0, 0)), fixed((T, D)), fixed((T, 128)),
            pl.BlockSpec((D, D), lambda s: (0, 3), pipeline_mode=pl.Buffered(1)),
            pl.BlockSpec((D, GW), lambda s: (0, s // 2)), fixed((NV, D)), fixed((8, D)), hbm(),
        ],
        out_specs=[
            fixed((SEQ, 2, D)), fixed((SEQ, 2, D)), fixed((24, 3 * D)), fixed((24, D)), fixed((24, FF)),
            *[pl.BlockSpec((w,), lambda s: (0,), pipeline_mode=pl.Buffered(1)) for w in VW],
        ],
        out_shape=[
            shape((SEQ, 2, D), BF), shape((SEQ, 2, D), BF), shape((24, 3 * D), F32), shape((24, D), F32),
            shape((24, FF), F32), *[shape((w,), F32) for w in VW],
        ],
        scratch_shapes=[
            pltpu.VMEM((T, D), BF), pltpu.VMEM((T, D), BF), pltpu.VMEM((T, GW), BF), pltpu.VMEM((T, D), F32),
            pltpu.VMEM((3, NZ, 2, 2, CH, GW), BF), pltpu.VMEM((NZ, 2, 2, CH, D), BF),
            pltpu.VMEM((N_UP, NZ, 2, 2, CH, HW), BF), *scatter_bufs(N_BACK, HW),
            pltpu.VMEM((N_BACK, CH, HW), F32), pltpu.VMEM((N_BACK, 24, HW), F32), pltpu.VMEM((10, 16, D), F32),
            *dma_sems(N_BACK * 7, N_BACK * 7, n_fin, n_fin, 6, 6, N_UP),
        ],
        compiler_params=pltpu.CompilerParams(collective_id=2, has_side_effects=True, vmem_limit_bytes=LIMIT),
        name="attention_back",
    )(x, yb, dx1, h1t, qkv, p, attn, rl, watt, watt, vec, sums, gup.reshape(NZ, 2, 2, CH, FF))


def by_pair(v):
    return v.reshape(v.shape[0], 3, 6, 128).transpose(0, 2, 1, 3).reshape(v.shape[0], 3 * D)


def by_kind(v):
    return v.reshape(v.shape[0], 6, 3, 128).transpose(0, 2, 1, 3).reshape(v.shape[0], 3 * D)


def with_own_copies(inputs, row_kind, w_qkv, w_out, w_up, w_down, vectors, b_up, out_grad):
    x, dm = inputs.transpose(1, 0, 2), out_grad.transpose(1, 0, 2)
    h1t, qkv, p, attn, rl, x1, dmp, h2t, g, slope, gdown, vec, watt, wup, down = forward(
        row_kind, x, dm, w_qkv, w_out, w_up, w_down, (*vectors, b_up))
    yb, dx1, gup, sums, gdown = ffn_back(
        x1, dmp, g, slope, wup.reshape(D, FF), down.reshape(FF, D), h2t, vec, gdown)
    out, gx, gqkv, gout, gup, *small = attn_back(
        x, yb, dx1, h1t, qkv, p, attn, rl, watt.reshape(D, UP_AT), vec, sums, gup)
    return out.transpose(1, 0, 2), gx.transpose(1, 0, 2), gqkv, gout, gup, gdown, small[:NV], small[NV]


def with_collectives(inputs, row_kind, w_qkv, w_out, w_up, w_down, vectors, b_up, out_grad):
    axes = ("dp", "fsdp")
    get = lambda v: lax.all_gather(v, axes, axis=0, tiled=True)
    wide = jnp.concatenate([by_pair(get(w_qkv)), get(w_out), get(w_up)], 1)
    down = get(w_down)
    full = [get(v).astype(F32) for v in vectors]
    vec = jnp.stack(full)
    bu = get(b_up).astype(F32)[None]
    bqkv = by_pair(jnp.concatenate([full[BQ], jnp.zeros_like(full[BQ]), full[BV]])[None])
    h1, qkv, p, attn, rl, x1 = attn_fwd(row_kind, inputs, wide, bqkv, vec)
    outputs, dx1, gup, gdown, gbu, gg2, gb2, gbd = ffn(x1, out_grad, wide, down, bu, vec)
    input_grad, gqkv, gout, gbqkv, gbo, gg1, gb1 = attn_bwd(inputs, dx1, h1, qkv, p, attn, rl, wide, vec)
    gbqkv = by_kind(gbqkv)
    small = [gg1, gb1, gbqkv[:, :D], gbqkv[:, 2 * D:], gbo, gg2, gb2, gbd]
    give = lambda v: lax.psum_scatter(v.astype(F32), axes, scatter_dimension=0, tiled=True)
    return (
        outputs, input_grad, give(by_kind(gqkv)), give(gout), give(gup), give(gdown),
        [give(v[0]) for v in small], give(gbu[0]),
    )


def on_device(
    copies, inputs, row_kind, ln1_gain, ln1_bias, w_qkv, b_query, b_value, w_out, b_out, ln2_gain, ln2_bias,
    w_up, b_up, w_down, b_down, out_grad,
):
    vectors = (ln1_gain, ln1_bias, b_query, b_value, b_out, ln2_gain, ln2_bias, b_down)
    run = with_own_copies if copies else with_collectives
    outputs, input_grad, gqkv, gout, gup, gdown, small, gbu = run(
        inputs, row_kind, w_qkv, w_out, w_up, w_down, vectors, b_up, out_grad)
    gg1, gb1, gbq, gbv, gbo, gg2, gb2, gbd = small
    return outputs, input_grad, gg1, gb1, gqkv, gbq, gbv, gout, gbo, gg2, gb2, gup, gbu, gdown, gbd


def solution(mesh):
    both = ("dp", "fsdp")
    row = P(both)
    mat = P(both, None)
    act = P(both, None, None)
    in_specs = (act, row, row, row, mat, row, row, mat, row, row, row, mat, row, mat, row, act)
    out_specs = (act, act, row, row, mat, row, row, mat, row, row, row, mat, row, mat, row)
    copies = mesh.shape["dp"] == 2 * NZ and mesh.shape["fsdp"] == 4
    return jax.shard_map(
        functools.partial(on_device, copies), mesh=mesh, in_specs=in_specs, out_specs=out_specs, check_vma=False
    )
```

time: 377 us -> 318 us (0.84); the launches traced: 377 us -> 313 us
  Pallas kernels: 351 us -> 299 us
  local copies, waits for them, and re-layouts: 23.7 us -> 12.4 us
    pallas_call x5 -> x3, Pallas kernels: 351 us -> 299 us  [the longest x1 124 us: forward(): pl.pallas_call(forward_kernel, grid=(N_ATT + N_UP,), in_specs=[pl.BlockSp...]
    concatenate x2 -> x0, local copies, waits for them, and re-layouts: 8.06 us -> none  [the longest x1 6.1 us: on_device(): small = jnp.concatenate([*vectors, b_up]).astype(F32)]
    unnamed x30 -> x43, local copies, waits for them, and re-layouts: 11.8 us -> 12.4 us
where the time goes in v2:
time: 318 us; the launch traced here: 313 us
  Pallas kernels  299 us (94%)
  local copies, waits for them, and re-layouts  12.4 us (4%)
    pallas_call x1, Pallas kernels, forward(): pl.pallas_call(forward_kernel, grid=(N_ATT + N_UP,), in_specs=[pl.BlockSp...  124 us
    pallas_call x1, Pallas kernels, attn_back(): pl.pallas_call(attn_back_kernel, grid=(N_ATT,), in_specs=[fixed((SEQ, 2,...  116 us
    pallas_call x1, Pallas kernels, ffn_back(): pl.pallas_call(ffn_back_kernel, grid=(N_UP,), in_specs=[fixed((T, D)), fi...  59.3 us
    unnamed x43, local copies, waits for them, and re-layouts  12.4 us

profile of v2, /device:TPU:0, one launch (start us, length us, event | category | flops | bytes accessed | tf_op | source)
XLA Modules:
  0.0 312.7 jit_solution(6277548989179200539)
XLA Ops:
  0.7 123.9 %forward.1 = (bf16[768,1088]{1,0:T(8,128)(2,1)}, bf16[1088,2304]{1,0:T(8,128)(2,1)}, bf16[2,12,544,544]{3,2,1,0:T(8,128)(2,1)}, bf16[1088,768]{1,0:T(8,128)(2,1)...) custom-call(s32[2]{0:T(128)} %kind_ref.1, ...), custom_call_target="tpu_custom_call" | custom-call | tf_op jit(solution)/shard_map/forward/pallas_call | solution.py:835
  124.5 59.3 %feed_forward_back.1 = (bf16[1088,768]{1,0:T(8,128)(2,1)}, f32[1088,768]{1,0:T(8,128)}, bf16[768,3072]{1,0:T(8,128)(2,1)}, f32[8,768]{1,0:T(8,128)}, f32[96,768]{1,0:T(8,128)}) custom-call(f32[1088,768]{1,0:T(8,128)} %get-tuple-element.49.x1_ref, bf16[1088,768]{1,0:T(8,128)(2,1)} %get-tuple-element.50.dm_ref, bf16[1088,3072]{1,0:T(8,128)(2,1)} %get-tuple-element.51.g_ref, ...), custom_call_target="tpu_custom_call" | custom-call | tf_op jit(solution)/shard_map/feed_forward_back/pallas_call | solution.py:946
  183.8 116.1 %attention_back.1 = (bf16[529,2,768]{2,1,0:T(2,128)(2,1)}, bf16[529,2,768]{2,1,0:T(2,128)(2,1)}, f32[24,2304]{1,0:T(8,128)}, f32[24,768]{1,0:T(8,128)}, f32[24,3...) custom-call(bf16[529,2,768]{2,1,0:T(2,128)(2,1)} %bitcast.13, ...), custom_call_target="tpu_custom_call" | custom-call | tf_op jit(solution)/shard_map/attention_back/pallas_call | solution.py:1205
  300.0 0.0 copy-start
  300.0 0.0 copy-start.13
  300.0 0.0 copy-start.12
  300.0 0.0 copy-start.3
  300.0 0.0 copy-start.11
  300.0 0.0 copy-start.10
  300.0 0.0 copy-start.4
  300.0 0.0 copy-start.9
  300.0 0.0 copy-start.8
  300.0 0.0 copy-start.7
  300.1 0.0 copy-start.2
  300.1 0.0 copy-start.6
  300.1 0.0 copy-start.1
  300.1 0.0 copy-start.5
  300.1 3.8 %copy.46 = bf16[2,529,768]{2,0,1:T(2,128)(2,1)} copy(bf16[2,529,768]{2,0,1:T(2,128)(2,1)} %bitcast.19) | data formatting | bytes 3250176
  303.9 0.0 copy-done
  303.9 1.2 copy.47
  305.1 0.0 copy-done.13
  305.1 0.5 copy.48
  305.6 0.0 copy-done.12
  305.6 0.5 copy.49
  306.1 0.0 copy-done.3
  306.1 0.7 copy.50
  306.8 0.0 copy-done.11
  306.8 0.5 copy.51
  307.3 0.0 copy-done.10
  307.3 0.5 copy.52
  307.9 0.0 copy-done.4
  307.9 0.6 copy.53
  308.5 0.0 copy-done.9
  308.5 0.5 copy.54
  309.0 0.0 copy-done.8
  309.0 0.5 copy.55
  309.5 0.0 copy-done.7
  309.5 0.5 copy.56
  310.0 0.0 copy-done.2
  310.0 0.7 copy.57
  310.8 0.0 copy-done.6
  310.8 0.5 copy.58
  311.3 0.0 copy-done.1
  311.3 0.7 copy.59
  312.0 0.0 copy-done.5
  312.0 0.5 copy.60
Async XLA Ops:
  300.0 4.0 %copy-start = (bf16[529,2,768]{2,1,0:T(2,128)(2,1)S(1)}, bf16[529,2,768]{2,1,0:T(2,128)(2,1)}, u32[]{:S(2)}) copy-start(bf16[529,2,768]{2,1,0:T(2,128)(2,1)} %get-tuple-element.69) | copy-start | bytes 4875268
  300.0 5.1 %copy-start.13 = (f32[24]{0:T(128)S(1)}, f32[24]{0:T(128)}, u32[]{:S(2)}) copy-start(f32[24]{0:T(128)} %get-tuple-element.100) | copy-start | bytes 292
  300.0 5.6 %copy-start.12 = (f32[24]{0:T(128)S(1)}, f32[24]{0:T(128)}, u32[]{:S(2)}) copy-start(f32[24]{0:T(128)} %get-tuple-element.101) | copy-start | bytes 292
  300.0 6.2 %copy-start.3 = (f32[24,2304]{1,0:T(8,128)S(1)}, f32[24,2304]{1,0:T(8,128)}, u32[]{:S(2)}) copy-start(f32[24,2304]{1,0:T(8,128)} %get-tuple-element.102) | copy-start | bytes 663556
  300.0 6.8 %copy-start.11 = (f32[24]{0:T(128)S(1)}, f32[24]{0:T(128)}, u32[]{:S(2)}) copy-start(f32[24]{0:T(128)} %get-tuple-element.103) | copy-start | bytes 292
  300.0 7.3 %copy-start.10 = (f32[24]{0:T(128)S(1)}, f32[24]{0:T(128)}, u32[]{:S(2)}) copy-start(f32[24]{0:T(128)} %get-tuple-element.104) | copy-start | bytes 292
  300.0 7.8 %copy-start.4 = (f32[24,768]{1,0:T(8,128)S(1)}, f32[24,768]{1,0:T(8,128)}, u32[]{:S(2)}) copy-start(f32[24,768]{1,0:T(8,128)} %get-tuple-element.105) | copy-start | bytes 221188
  300.0 8.5 %copy-start.9 = (f32[24]{0:T(128)S(1)}, f32[24]{0:T(128)}, u32[]{:S(2)}) copy-start(f32[24]{0:T(128)} %get-tuple-element.106) | copy-start | bytes 292
  300.0 9.0 %copy-start.8 = (f32[24]{0:T(128)S(1)}, f32[24]{0:T(128)}, u32[]{:S(2)}) copy-start(f32[24]{0:T(128)} %get-tuple-element.107) | copy-start | bytes 292
  300.0 9.5 %copy-start.7 = (f32[24]{0:T(128)S(1)}, f32[24]{0:T(128)}, u32[]{:S(2)}) copy-start(f32[24]{0:T(128)} %get-tuple-element.108) | copy-start | bytes 292
  300.1 10.0 %copy-start.2 = (f32[24,3072]{1,0:T(8,128)S(1)}, f32[24,3072]{1,0:T(8,128)}, u32[]{:S(2)}) copy-start(f32[24,3072]{1,0:T(8,128)} %get-tuple-element.109) | copy-start | bytes 884740
  300.1 10.7 %copy-start.6 = (f32[96]{0:T(128)S(1)}, f32[96]{0:T(128)}, u32[]{:S(2)}) copy-start(f32[96]{0:T(128)} %get-tuple-element.110) | copy-start | bytes 1156
  300.1 11.2 %copy-start.1 = (f32[96,768]{1,0:T(8,128)S(1)}, f32[96,768]{1,0:T(8,128)}, u32[]{:S(2)}) copy-start(f32[96,768]{1,0:T(8,128)} %get-tuple-element.111) | copy-start | bytes 884740
  300.1 11.9 %copy-start.5 = (f32[24]{0:T(128)S(1)}, f32[24]{0:T(128)}, u32[]{:S(2)}) copy-start(f32[24]{0:T(128)} %get-tuple-element.112) | copy-start | bytes 292
